TPU v7x, 256 devices: a whole 4x4x8 slice. The times are simulated.
256 devices in a mesh: dom: 16 (over x, y_lo, core), grp: 16 (over z, y_hi).
Axes of the slice: x: 4, y: 4 (y_hi: 2, y_lo: 2; y = y_hi * 2 + y_lo), z: 8, core: 2. Of those that a mesh axis runs over, the one named last changes fastest.
Arguments:
- interface_panel: bfloat16 [4096, 512], P('dom'), may hold values from -6 to 6
- interface_block: bfloat16 [4096, 256], P('dom'), may hold values from -0.375 to 0.375
- coupling: bfloat16 [16, 16384, 4096], P('dom', 'grp'), may hold values from -0.09375 to 0.09375
- coupling_pattern: int32 [16, 32, 16], P('dom', 'grp'), may hold values from 0 to 1, as said below
- tile_ranks: int32 [16, 32], P('dom', 'grp'), may hold values from 16 to 64
- basis_left: bfloat16 [16, 64, 16384], P('dom', None, 'grp'), may hold values from -0.75 to 0.75
- basis_right: bfloat16 [16, 64, 16384], P('dom', None, 'grp'), may hold values from -0.046875 to 0.046875
- interior_scale: float32 [16, 16384], P('dom', 'grp'), may hold values from 0.5 to 2
Outputs:
- schur_image: float32 [4096, 512], P('dom')
Inputs may be any that keep to these rules, and one draw needn't show every extreme that they name: `coupling_pattern`: each subdomain couples every tile to its own interface block; subdomains differ in how many blocks their tiles couple to.
All inputs are finite; a program needn't handle non-finite values.
Results may differ from a plain program's by a relative error of at most 0.00047.
Values may be sent and summed in bfloat16 or wider, within the bound.
No kernel may reach another device: no remote copies, remote signals or barrier semaphores. Data moves between devices by JAX's collectives and lax.ppermute only.
A program may use at most 64 MiB of HBM per device.

v0:
```python
import functools

import jax
import jax.numpy as jnp
from jax import lax
from jax.experimental import pallas as pl
from jax.experimental.pallas import tpu as pltpu
from jax.sharding import PartitionSpec as P

TILE = 512
RANK = 64
BLOCK = 256
TILES = 2
SLAB = 256
BF16 = jnp.bfloat16
F32 = jnp.float32
VMEM_BYTES = 20 * 1024 * 1024


def split3(value):
    high = value.astype(BF16)
    rest = value - high.astype(F32)
    middle = rest.astype(BF16)
    low = (rest - middle.astype(F32)).astype(BF16)
    return high, middle, low


def rank_masked(basis, rank):
    row = lax.broadcasted_iota(jnp.int32, basis.shape, 0)
    return jnp.where(row < rank, basis, jnp.zeros_like(basis))


STEPS = ((0, 0), (0, 1), (-1, 0), (1, 0), (2, 0), (-1, 1), (1, 1), (2, 1))


def owned_block(step, same_core):
    wide, high = lax.axis_size("x"), lax.axis_size("yl")
    x = lax.rem(lax.axis_index("x") + (step[0] + wide), wide)
    y = lax.rem(lax.axis_index("yl") + (step[1] + high), high)
    core = lax.axis_index("c")
    return (x * high + y) * 2 + (core if same_core else 1 - core)


def mask_kernel(pattern_ref, ranks_ref, coupling_ref, right_ref, left_ref, *refs, tile, last):
    own_ref, other_ref, left_out_ref, *fold_out_refs, fold_ref = refs[-6:] if last else refs[-5:]
    step = pl.program_id(0)
    left = rank_masked(left_ref[...], ranks_ref[tile])
    left_out_ref[...] = jnp.concatenate([left] * 3, axis=0)
    right = rank_masked(right_ref[...], ranks_ref[tile])

    @pl.when(step == 0)
    def _():
        fold_ref[...] = refs[0][...] if last else jnp.zeros_like(fold_ref)

    for index, out_ref in enumerate((own_ref, other_ref)):
        for k in range(out_ref.shape[1] // BLOCK):
            block = owned_block(STEPS[k], index == 0)
            columns = coupling_ref[:, pl.ds(pl.multiple_of(block * BLOCK, BLOCK), BLOCK)]
            keep = pattern_ref[tile, block].astype(F32)
            keep = jnp.broadcast_to(keep, columns.shape).astype(BF16)
            out_ref[:, k * BLOCK : (k + 1) * BLOCK] = columns * keep
        fold_ref[index] += jnp.dot(right, out_ref[...], preferred_element_type=F32)

    @pl.when(step == pl.num_programs(0) - 1)
    def _():
        if last:
            for index, out_ref in enumerate(fold_out_refs):
                out_ref[...] = jnp.concatenate(split3(fold_ref[index]), axis=0)
        else:
            fold_out_refs[0][...] = fold_ref[...]


def stacked(refs):
    return jnp.concatenate([ref[...] for ref in refs], axis=0)


def member():
    return lax.rem(lax.axis_index("z"), 2) * 2 + lax.axis_index("yh")


def portion_rows(change, count):
    place = member()
    place = place + (change & 1) * (1 - 2 * lax.rem(place, 2))
    place = place + (change & 2) * (1 - 2 * lax.div(place, 2))
    return pl.ds(pl.multiple_of(place * count, count), count)


def project_kernel(own_fold_ref, other_fold_ref, *refs):
    panel_refs, out_refs, total_ref = refs[:-5], refs[-5:-1], refs[-1]
    half = len(panel_refs) // 2
    value = jnp.dot(own_fold_ref[...], stacked(panel_refs[:half]), preferred_element_type=F32)
    value += jnp.dot(
        other_fold_ref[...], stacked(panel_refs[half:]), preferred_element_type=F32
    )
    total_ref[...] = value[:RANK] + (value[RANK : 2 * RANK] + value[2 * RANK :])
    for change, out_ref in enumerate(out_refs):
        out_ref[...] = total_ref[portion_rows(change, out_ref.shape[0]), :]


def load_first_kernel(*refs):
    masked_refs, refs = refs[:TILES], refs[TILES:]
    out_ref, token_ref = refs[-2:]
    token_ref[...] = jnp.zeros_like(token_ref)
    panel = stacked(refs[:-2])
    for tile in range(out_ref.shape[0] // TILE):
        rows = slice(tile * TILE, (tile + 1) * TILE)
        out_ref[rows, :] = jnp.dot(masked_refs[tile][...], panel, preferred_element_type=F32)


def load_second_kernel(first_ref, scale_ref, *refs):
    masked_refs, refs = refs[:TILES], refs[TILES:]
    out_ref, token_ref = refs[-2:]
    token_ref[...] = jnp.zeros_like(token_ref)
    panel = stacked(refs[:-2])
    for tile in range(first_ref.shape[0] // TILE):
        rows = slice(tile * TILE, (tile + 1) * TILE)
        load = jnp.dot(masked_refs[tile][...], panel, preferred_element_type=F32)
        out_ref[:, rows] = scale_ref[:, rows] * (first_ref[rows, :] + load).T


def back_block(solved_ref, masked_refs, block):
    columns = slice(block * BLOCK, (block + 1) * BLOCK)
    masked = jnp.concatenate([ref[:, columns] for ref in masked_refs], axis=0)
    return jnp.dot(solved_ref[...], masked, preferred_element_type=F32)


def solve_back_kernel(scaled_ref, *refs):
    left_refs, masked_refs, part_refs = refs[:TILES], refs[TILES : 2 * TILES], refs[2 * TILES : -3]
    solved_ref, out_ref, projection_ref = refs[-3:]
    for change, part_ref in enumerate(part_refs):
        projection_ref[portion_rows(change, part_ref.shape[0]), :] = part_ref[...]
    pieces = jnp.concatenate(split3(projection_ref[...]), axis=0)
    for tile, left_ref in enumerate(left_refs):
        low_rank = lax.dot_general(
            pieces, left_ref[...], (((0,), (0,)), ((), ())), preferred_element_type=F32
        )
        rows = slice(tile * TILE, (tile + 1) * TILE)
        solved_ref[:, rows] = (scaled_ref[:, rows] + low_rank).astype(BF16)
    for k in range(out_ref.shape[0]):
        out_ref[k] = back_block(solved_ref, masked_refs, k).astype(BF16)


def back_kernel(solved_ref, *refs, start):
    masked_refs, out_ref = refs[:TILES], refs[-1]
    for k in range(out_ref.shape[0]):
        out_ref[k] = back_block(solved_ref, masked_refs, start + k).astype(BF16)


def back_add_kernel(solved_ref, *refs, start):
    masked_refs, given_ref, out_ref = refs[:TILES], refs[TILES], refs[-1]
    for k in range(given_ref.shape[0]):
        value = back_block(solved_ref, masked_refs, start + k) + given_ref[k].astype(F32)
        owner = lax.div(owned_block(STEPS[start + k], True), 2)
        out_ref[owner] = value.astype(BF16)


def params():
    return pltpu.CompilerParams(vmem_limit_bytes=VMEM_BYTES)


def cost(flops, size):
    return pl.CostEstimate(flops=flops, bytes_accessed=size, transcendentals=0)


def whole(shape):
    return pl.BlockSpec(shape, lambda *_: (0,) * len(shape), pipeline_mode=pl.Buffered(1))


ANYWHERE = pl.BlockSpec(memory_space=pl.ANY)
INSIDE = pl.BlockSpec(memory_space=pltpu.VMEM)


def far(value):
    return pltpu.with_memory_space_constraint(value, pltpu.HBM)


def near_by(value):
    return pltpu.with_memory_space_constraint(value, pltpu.VMEM)


def mask(pattern, ranks, coupling, right, left, tile, fold=None, after=None):
    rows, width = coupling.shape
    half = width // 2
    steps = TILE // SLAB
    last = fold is not None
    masked = jax.ShapeDtypeStruct((TILE, half), BF16)
    masked_spec = pl.BlockSpec((SLAB, half), lambda i, *_: (i, 0))
    basis_spec = pl.BlockSpec((RANK, SLAB), lambda i, *_: (0, tile * steps + i))
    if last:
        folds = [jax.ShapeDtypeStruct((3 * RANK, half), BF16)] * 2
    else:
        folds = [jax.ShapeDtypeStruct((2, RANK, half), F32)]
    more = [fold, after] if last else []
    return pl.pallas_call(
        functools.partial(mask_kernel, tile=tile, last=last),
        out_shape=[masked, masked, jax.ShapeDtypeStruct((3 * RANK, TILE), BF16)] + folds,
        grid_spec=pltpu.PrefetchScalarGridSpec(
            num_scalar_prefetch=2,
            grid=(steps,),
            in_specs=[
                pl.BlockSpec((SLAB, width), lambda i, *_: (tile * steps + i, 0)),
                basis_spec,
                basis_spec,
            ]
            + ([whole(fold.shape), ANYWHERE] if last else []),
            out_specs=[
                masked_spec, masked_spec, pl.BlockSpec((3 * RANK, SLAB), lambda i, *_: (0, i))
            ]
            + [whole(shape.shape) for shape in folds],
            scratch_shapes=[pltpu.VMEM((2, RANK, half), F32)],
        ),
        cost_estimate=cost(2 * TILE * width * RANK, 4 * TILE * width),
        compiler_params=params(),
        name="mask",
    )(far(pattern), far(ranks), far(coupling), far(right), far(left), *more)


def inside(kernel, name, out_shape, operands, flops, aliases=None, scratch=()):
    return pl.pallas_call(
        kernel,
        out_shape=out_shape,
        in_specs=[INSIDE] * len(operands),
        out_specs=jax.tree.map(lambda _: INSIDE, out_shape),
        scratch_shapes=scratch,
        input_output_aliases=aliases or {},
        cost_estimate=cost(flops, 1 << 20),
        compiler_params=params(),
        name=name,
    )(*[near_by(operand) for operand in operands])


def project(own_fold, other_fold, mine, theirs):
    vectors = mine[0].shape[1]
    part = jax.ShapeDtypeStruct((RANK // 4, vectors), F32)
    return inside(
        project_kernel, "project", [part] * 4, (own_fold, other_fold, *mine, *theirs),
        12 * own_fold.size * vectors, None, [pltpu.VMEM((RANK, vectors), F32)],
    )


def load_first(masked, panels):
    rows, depth = len(masked) * TILE, masked[0].shape[1]
    vectors = panels[0].shape[1]
    out = jax.ShapeDtypeStruct((rows, vectors), F32)
    token = jax.ShapeDtypeStruct((RANK // 4, vectors), F32)
    return inside(
        load_first_kernel, "load_first", (out, token), (*masked, *panels),
        2 * rows * depth * vectors,
    )


def load_second(masked, panels, first, scale):
    rows, depth = len(masked) * TILE, masked[0].shape[1]
    vectors = panels[0].shape[1]
    out = jax.ShapeDtypeStruct((vectors, rows), F32)
    token = jax.ShapeDtypeStruct((RANK // 4, vectors), F32)
    return inside(
        load_second_kernel, "load_second", (out, token), (first, scale, *masked, *panels),
        2 * rows * depth * vectors,
    )


def solve_back(scaled, parts, left, masked, count):
    vectors, rows = scaled.shape
    out = (
        jax.ShapeDtypeStruct((vectors, rows), BF16),
        jax.ShapeDtypeStruct((count, vectors, BLOCK), BF16),
    )
    return inside(
        solve_back_kernel, "solve_back", out, (scaled, *left, *masked, *parts),
        2 * rows * count * BLOCK * vectors, None, [pltpu.VMEM((RANK, vectors), F32)],
    )


def back(solved, masked, start, count):
    vectors, rows = solved.shape
    return inside(
        functools.partial(back_kernel, start=start), "back",
        jax.ShapeDtypeStruct((count, vectors, BLOCK), BF16), (solved, *masked),
        2 * rows * count * BLOCK * vectors,
    )


def back_add(solved, masked, start, given, into):
    vectors, rows = solved.shape
    return inside(
        functools.partial(back_add_kernel, start=start), "back_add",
        jax.ShapeDtypeStruct((len(STEPS), vectors, BLOCK), BF16),
        (solved, *masked, given, *into), 2 * rows * given.shape[0] * BLOCK * vectors,
        {2 + TILES: 0} if into else None,
    )


def exchange(value, axes):
    return lax.all_to_all(value, axes, 0, 0, tiled=True)


def swap(value):
    return lax.ppermute(value, "c", [(0, 1), (1, 0)])


def pin_kernel(*refs):
    pass


def pin(values, after):
    shapes = [jax.ShapeDtypeStruct(value.shape, value.dtype) for value in values]
    return pl.pallas_call(
        pin_kernel,
        out_shape=shapes,
        in_specs=[ANYWHERE] * (len(values) + 1),
        out_specs=[ANYWHERE] * len(values),
        input_output_aliases={k: k for k in range(len(values))},
        compiler_params=params(),
        name="pin",
    )(*values, after)


def shift(value, dx, dy, dh=0):
    wide, high, halves = [lax.axis_size(name) for name in ("x", "yl", "yh")]
    pairs = [
        (
            (x * high + y) * halves + h,
            ((x + dx) % wide * high + (y + dy) % high) * halves + (h + dh) % halves,
        )
        for x in range(wide)
        for y in range(high)
        for h in range(halves)
    ]
    return lax.ppermute(value, ("x", "yl", "yh"), pairs)


NEAR = ((0, 1), (1, 0), (1, 1))
APART = ((2, 0), (4, 0), (6, 0))


def trade(values, partners):
    layers, halves = lax.axis_size("z"), lax.axis_size("yh")
    received = []
    for value, (dz, dh) in zip(values, partners):
        pairs = [
            (z * halves + h, (z ^ dz) * halves + (h ^ dh))
            for z in range(layers)
            for h in range(halves)
        ]
        received.append(lax.ppermute(value, ("z", "yh"), pairs))
    return received


def total(value, terms, token):
    return (value + terms[0]) + (terms[1] + terms[2]) + token


def local(
    interface_panel,
    interface_block,
    coupling,
    coupling_pattern,
    tile_ranks,
    basis_left,
    basis_right,
    interior_scale,
):
    members = lax.axis_size("z") * lax.axis_size("yh")
    block_rows, vectors = interface_panel.shape
    here = interface_panel
    across, beside = shift(here, 2, 0), shift(here, 0, 1)
    behind, ahead = shift(here, 1, 0), shift(here, -1, 0)
    rest = tile_ranks[0], coupling[0], basis_right[0], basis_left[0]
    own_0, other_0, left_0, fold = mask(coupling_pattern[0], *rest, 0)
    across, beside = pin([across, beside], fold)
    corners = [shift(beside, 1, 0), shift(beside, -1, 0), shift(across, 0, 1, 1)]
    own_1, other_1, left_1, own_fold, other_fold = mask(
        coupling_pattern[0], *rest, 1, fold, beside
    )
    own, other, left = (own_0, own_1), (other_0, other_1), (left_0, left_1)
    mine = [*pin([here, beside, behind, ahead, across], left_1), *corners]
    theirs = [swap(block) for block in mine]
    keep, *others = project(own_fold, other_fold, mine, theirs)
    received = trade(others, NEAR)
    first, token_1 = load_first(own, mine)
    scaled, token_2 = load_second(other, theirs, first, interior_scale)
    keep = total(keep, received, token_1)
    keep = total(keep, trade([keep] * 3, APART), token_2)
    parts = [keep] + trade([keep] * 3, NEAR)

    half = len(STEPS) // 2
    solved, give = solve_back(scaled, parts, left, other, half)
    give_1 = swap(give)
    give_2 = swap(back(solved, other, half, half))
    term = back_add(solved, own, 0, give_1, ())
    term = back_add(solved, own, half, give_2, (term,))

    halves, layers = lax.axis_size("yh"), lax.axis_size("z")
    part, piece = vectors // halves, vectors // members
    term = term.reshape(len(STEPS) * halves, part, block_rows)
    term = jnp.sum(exchange(term, ("x", "yl", "yh")).astype(F32), axis=0)
    term = jnp.sum(exchange(term.reshape(layers, piece, block_rows), "z"), axis=0)
    term = exchange(jnp.broadcast_to(term[None], (members, piece, block_rows)), ("yh", "z"))
    coupled = term.reshape(vectors, block_rows).T
    local_image = jnp.dot(interface_block, interface_panel, preferred_element_type=F32)
    return local_image - coupled


def solution(mesh):
    shape = (4, 2, 2, 8, 2)
    fine = jax.sharding.Mesh(mesh.devices.reshape(shape), ("x", "yl", "c", "z", "yh"))
    dom, grp = ("x", "yl", "c"), ("z", "yh")
    return jax.shard_map(
        local,
        mesh=fine,
        in_specs=(
            P(dom, None),
            P(dom, None),
            P(dom, grp, None),
            P(dom, grp, None),
            P(dom, grp),
            P(dom, None, grp),
            P(dom, None, grp),
            P(dom, grp),
        ),
        out_specs=P(dom, None),
        check_vma=False,
    )
```

profile of v0, /device:TPU:32, one launch (start us, length us, event | category | flops | bytes accessed | tf_op | source)
XLA Modules:
  0.0 135.2 jit_solution(870285222900572882)
XLA Ops:
  0.0 3.0 %collective-permute-start = (bf16[256,512]{1,0:T(8,128)(2,1)}, bf16[256,512]{1,0:T(8,128)(2,1)S(1)}, u32[]{:S(2)}, u32[]{:S(2)}) collective-permute-start(bf16[256,512]{1,0:T(8,128)(2,1)} %param.8), channel_id=1, source_target_pairs={{0,128},{1,129},{32,160},{33,161},{64,192},{65,193},{96,224},{97,2... | collective-permute-start | bytes 786440 | tf_op jit(solution)/shard_map/ppermute | solution.py:330
  3.0 1.6 %collective-permute-start.1 = (bf16[256,512]{1,0:T(8,128)(2,1)}, bf16[256,512]{1,0:T(8,128)(2,1)S(1)}, u32[]{:S(2)}, u32[]{:S(2)}) collective-permute-start(bf16[256,512]{1,0:T(8,128)(2,1)} %param.8), channel_id=1, source_target_pairs={{0,32},{1,33},{32,0},{33,1},{64,96},{65,97},{96,64},{97,65},{128,1... | collective-permute-start | bytes 786440 | tf_op jit(solution)/shard_map/ppermute | solution.py:330
  4.6 0.6 collective-permute-start.2
  5.2 2.6 %collective-permute-start.3 = (bf16[256,512]{1,0:T(8,128)(2,1)}, bf16[256,512]{1,0:T(8,128)(2,1)S(1)}, u32[]{:S(2)}, u32[]{:S(2)}) collective-permute-start(bf16[256,512]{1,0:T(8,128)(2,1)} %param.8), channel_id=1, source_target_pairs={{0,192},{1,193},{32,224},{33,225},{64,0},{65,1},{96,32},{97,33},{1... | collective-permute-start | bytes 786440 | tf_op jit(solution)/shard_map/ppermute | solution.py:330
  7.8 4.0 %mask.2 = (bf16[512,2048]{1,0:T(8,128)(2,1)S(1)}, bf16[512,2048]{1,0:T(8,128)(2,1)S(1)}, bf16[192,512]{1,0:T(8,128)(2,1)S(1)}, f32[2,64,2048]{2,1,0:T(8,128)S(1)}) custom-call(s32[2,16]{1,0:T(2,128)} %bitcast.21, s32[2]{0:T(128)} %bitcast.23, bf16[1024,4096]{1,0:T(8,128)(2,1)} %bitcast.13, bf16[64,1024]{1,0:T(8,128)(2,1)} %bitcast.17, bf16[64,1024]{1,0:T(8,128)(2,1)} %bitcast.19), custom_call_target="tpu_custom_call" | custom-call | flops 268435456 | bytes 8388608 | tf_op jit(solution)/shard_map/mask/pallas_call | solution.py:194
  11.8 0.0 collective-permute-done.refs_0_
  11.9 0.0 collective-permute-done.1.refs_1_
  11.9 0.6 collective-permute-start.4
  12.5 2.7 %collective-permute-start.5 = (bf16[256,512]{1,0:T(8,128)(2,1)S(1)}, bf16[256,512]{1,0:T(8,128)(2,1)S(1)}, u32[]{:S(2)}, u32[]{:S(2)}) collective-permute-start(bf16[256,512]{1,0:T(8,128)(2,1)S(1)} %get-tuple-element.33.refs_1_), channel_id=1, source_target_pairs={{0,192},{1,193},{32,224},{33,225},{64,0},{65,1},{96,32},{97,33},{1... | collective-permute-start | bytes 786440 | tf_op jit(solution)/shard_map/ppermute | solution.py:330
  15.2 2.1 %collective-permute-start.6 = (bf16[256,512]{1,0:T(8,128)(2,1)S(1)}, bf16[256,512]{1,0:T(8,128)(2,1)S(1)}, u32[]{:S(2)}, u32[]{:S(2)}) collective-permute-start(bf16[256,512]{1,0:T(8,128)(2,1)S(1)} %get-tuple-element.35.refs_4_), channel_id=1, source_target_pairs={{0,33},{1,32},{32,1},{33,0},{64,97},{65,96},{96,65},{97,64},{128,1... | collective-permute-start | bytes 786440 | tf_op jit(solution)/shard_map/ppermute | solution.py:330
  17.4 4.1 %mask.3 = (bf16[512,2048]{1,0:T(8,128)(2,1)S(1)}, bf16[512,2048]{1,0:T(8,128)(2,1)S(1)}, bf16[192,512]{1,0:T(8,128)(2,1)S(1)}, bf16[192,2048]{1,0:T(8,128)(2,1)S(1)}, bf16[192,2048]{1,0:T(8,128)(2,1)S(1)}) custom-call(s32[2,16]{1,0:T(2,128)} %bitcast.22, s32[2]{0:T(128)} %bitcast.24, bf16[1024,4096]{1,0:T(8,128)(2,1)} %bitcast.14, ...), custom_call_target="tpu_custom_call" | custom-call | flops 268435456 | bytes 8388608 | tf_op jit(solution)/shard_map/mask/pallas_call | solution.py:194
  21.5 0.0 collective-permute-done.2.refs_2_
  21.5 0.0 collective-permute-done.5.refs_8_.refs_6_
  21.5 1.3 collective-permute-done.6.refs_9_.refs_7_
  22.8 0.0 collective-permute-start.10
  22.8 0.5 collective-permute-start.11
  23.3 0.0 collective-permute-start.7
  23.3 0.5 collective-permute-start.8
  23.8 0.0 collective-permute-start.9
  23.8 0.5 collective-permute-done.10.refs_5_.refs_11_
  24.3 0.1 collective-permute-start.12
  24.5 0.2 collective-permute-done.11.refs_6_.refs_12_
  24.7 0.1 collective-permute-start.13
  24.8 0.2 collective-permute-done.7.refs_2_.refs_8_
  25.1 0.1 collective-permute-start.14
  25.2 0.2 collective-permute-done.8.refs_3_.refs_9_
  25.4 0.4 collective-permute-done.9.refs_4_.refs_10_
  25.8 0.4 collective-permute-done.12.refs_7_.refs_13_
  26.2 0.4 collective-permute-done.13.refs_8_.refs_14_
  26.6 0.4 collective-permute-done.14.refs_9_.refs_15_
  26.9 1.0 project.1
  27.9 1.8 %collective-permute-start.15 = (f32[16,512]{1,0:T(8,128)S(1)}, f32[16,512]{1,0:T(8,128)S(1)}, u32[]{:S(2)}, u32[]{:S(2)}) collective-permute-start(f32[16,512]{1,0:T(8,128)S(1)} %get-tuple-element.50), channel_id=1, source_target_pairs={{0,1},{1,0},{2,3},{3,2},{4,5},{5,4},{6,7},{7,6},{8,9},{9,8},{10,11... | collective-permute-start | bytes 98312 | tf_op jit(solution)/shard_map/ppermute | solution.py:346
  29.7 0.1 collective-permute-start.16
  29.8 3.2 %collective-permute-start.17 = (f32[16,512]{1,0:T(8,128)S(1)}, f32[16,512]{1,0:T(8,128)S(1)}, u32[]{:S(2)}, u32[]{:S(2)}) collective-permute-start(f32[16,512]{1,0:T(8,128)S(1)} %get-tuple-element.52), channel_id=1, source_target_pairs={{0,3},{1,2},{2,1},{3,0},{4,7},{5,6},{6,5},{7,4},{8,11},{9,10},{10,... | collective-permute-start | bytes 98312 | tf_op jit(solution)/shard_map/ppermute | solution.py:346
  33.0 2.4 %load_first.1 = (f32[1024,512]{1,0:T(8,128)S(1)}, f32[16,512]{1,0:T(8,128)S(1)}) custom-call(bf16[512,2048]{1,0:T(8,128)(2,1)S(1)} %get-tuple-element.31.refs_0_, bf16[512,2048]{1,0:T(8,128)(2,1)S(1)} %get-tuple-element.34.refs_1_, bf16[256,512]{1,0:T(8,128)(2,1)S(1)} %get-tuple-element.37.refs_2_.refs_0_, ...), custom_call_target="tpu_custom_call" | custom-call | flops 2147483648 | bytes 1048576 | tf_op jit(solution)/shard_map/load_first/pallas_call | solution.py:219
  35.4 0.0 collective-permute-done.15
  35.4 0.0 collective-permute-done.16
  35.4 0.7 collective-permute-done.17
  36.2 3.4 %collective-permute-start.18 = (f32[16,512]{1,0:T(8,128)S(1)}, f32[16,512]{1,0:T(8,128)S(1)}, u32[]{:S(2)}, u32[]{:S(2)}) collective-permute-start(f32[16,512]{1,0:T(8,128)S(1)} %add_add_fusion.1), channel_id=1, source_target_pairs={{0,4},{1,5},{2,6},{3,7},{4,0},{5,1},{6,2},{7,3},{8,12},{9,13},{10,... | collective-permute-start | bytes 98312 | tf_op jit(solution)/shard_map/ppermute | solution.py:346
  39.5 5.4 %collective-permute-start.19 = (f32[16,512]{1,0:T(8,128)S(1)}, f32[16,512]{1,0:T(8,128)S(1)}, u32[]{:S(2)}, u32[]{:S(2)}) collective-permute-start(f32[16,512]{1,0:T(8,128)S(1)} %add_add_fusion.1), channel_id=1, source_target_pairs={{0,8},{1,9},{2,10},{3,11},{4,12},{5,13},{6,14},{7,15},{8,0},{9,1},... | collective-permute-start | bytes 98312 | tf_op jit(solution)/shard_map/ppermute | solution.py:346
  44.9 2.6 %load_second.1 = (f32[512,1024]{1,0:T(8,128)S(1)}, f32[16,512]{1,0:T(8,128)S(1)}) custom-call(f32[1024,512]{1,0:T(8,128)S(1)} %get-tuple-element.42.first_ref, f32[1,1024]{1,0:T(1,128)S(1)} %copy-done.1, bf16[512,2048]{1,0:T(8,128)(2,1)S(1)} %get-tuple-element.43.refs_0_.refs_2_, bf16[512,2048]{1,0:T(8,128)(2,1)S(1)} %get-tuple-element.44.refs_1_.refs_3_, ...), custom_call_target="tpu_custom_call" | custom-call | flops 2147483648 | bytes 1048576 | tf_op jit(solution)/shard_map/load_second/pallas_call | solution.py:219
  47.5 0.0 collective-permute-done.18
  47.5 0.1 collective-permute-done.19
  47.6 3.3 %collective-permute-done.20 = f32[16,512]{1,0:T(8,128)S(1)} collective-permute-done((f32[16,512]{1,0:T(8,128)S(1)}, f32[16,512]{1,0:T(8,128)S(1)}, u32[]{:S(2)}, u32[]{:S(2)}) %collective-permute-start.20) | collective-permute-done | bytes 32800 | tf_op jit(solution)/shard_map/ppermute | solution.py:346
  51.0 1.9 %collective-permute-start.21 = (f32[16,512]{1,0:T(8,128)S(1)}, f32[16,512]{1,0:T(8,128)S(1)}, u32[]{:S(2)}, u32[]{:S(2)}) collective-permute-start(f32[16,512]{1,0:T(8,128)S(1)} %add_add_fusion.refs_4_), channel_id=1, source_target_pairs={{0,1},{1,0},{2,3},{3,2},{4,5},{5,4},{6,7},{7,6},{8,9},{9,8},{10,11... | collective-permute-start | bytes 98312 | tf_op jit(solution)/shard_map/ppermute | solution.py:346
  52.9 1.0 collective-permute-start.22
  53.9 2.1 %collective-permute-start.23 = (f32[16,512]{1,0:T(8,128)S(1)}, f32[16,512]{1,0:T(8,128)S(1)}, u32[]{:S(2)}, u32[]{:S(2)}) collective-permute-start(f32[16,512]{1,0:T(8,128)S(1)} %add_add_fusion.refs_4_), channel_id=1, source_target_pairs={{0,3},{1,2},{2,1},{3,0},{4,7},{5,6},{6,5},{7,4},{8,11},{9,10},{10,... | collective-permute-start | bytes 98312 | tf_op jit(solution)/shard_map/ppermute | solution.py:346
  56.0 0.4 collective-permute-done.21.refs_5_
  56.5 0.3 collective-permute-done.22.refs_6_
  56.8 3.4 %collective-permute-done.23.refs_7_ = f32[16,512]{1,0:T(8,128)S(1)} collective-permute-done((f32[16,512]{1,0:T(8,128)S(1)}, f32[16,512]{1,0:T(8,128)S(1)}, u32[]{:S(2)}, u32[]{:S(2)}) %collective-permute-start.23) | collective-permute-done | bytes 32800 | tf_op jit(solution)/shard_map/ppermute | solution.py:346
  60.2 1.6 %solve_back.1 = (bf16[512,1024]{1,0:T(8,128)(2,1)S(1)}, bf16[4,512,256]{2,1,0:T(8,128)(2,1)S(1)}) custom-call(f32[512,1024]{1,0:T(8,128)S(1)} %get-tuple-element.45.scaled_ref, bf16[192,512]{1,0:T(8,128)(2,1)S(1)} %get-tuple-element.46.refs_0_, bf16[192,512]{1,0:T(8,128)(2,1)S(1)} %get-tuple-element.36.refs_5_.refs_1_, ...), custom_call_target="tpu_custom_call" | custom-call | flops 1073741824 | bytes 1048576 | tf_op jit(solution)/shard_map/solve_back/pallas_call | solution.py:219
  61.8 0.1 collective-permute-start.25
  61.9 1.2 back.1
  63.2 0.6 collective-permute-start.24
  63.8 0.8 collective-permute-done.25.refs_2_
  64.6 1.3 back_add.2.refs_3_
  65.9 0.2 collective-permute-done.24.refs_2_
  66.1 1.3 back_add.3
  67.4 33.9 %all_to_all.15 = bf16[16,256,256]{2,1,0:T(8,128)(2,1)S(1)} all-to-all(bf16[16,256,256]{2,1,0:T(8,128)(2,1)S(1)} %bitcast.12), channel_id=1, replica_groups=mesh['x'=4,'yl'=2,'c'=2,'z'=8,'yh'=2] {'x','yl','yh'}, dimensions={0} | all-to-all | bytes 4194304 | tf_op jit(solution)/shard_map/all_to_all | solution.py:295
  101.3 0.3 convert_reduce_fusion
  101.6 13.7 %all_to_all.16 = f32[8,32,256]{2,1,0:T(8,128)S(1)} all-to-all(f32[8,32,256]{2,1,0:T(8,128)S(1)} %bitcast.16), channel_id=1, replica_groups=mesh['x'=4,'yl'=2,'c'=2,'z'=8,'yh'=2] {'z'}, dimensions={0} | all-to-all | bytes 524288 | tf_op jit(solution)/shard_map/all_to_all | solution.py:295
  115.3 18.6 %all_to_all.17 = f32[16,32,256]{2,1,0:T(8,128)S(1)} all-to-all(f32[16,32,256]{2,1,0:T(8,128)S(1)} %broadcast_in_dim.2), channel_id=1, replica_groups=mesh['x'=4,'yl'=2,'c'=2,'z'=8,'yh'=2] {'yh','z'}, dimensions={0} | all-to-all | bytes 1048576 | tf_op jit(solution)/shard_map/all_to_all | solution.py:295
  133.9 0.2 copy.18
  134.2 1.0 convolution_subtract_fusion
  (16 shorter events, 0.1 us)
Async XLA Ops:
  0.0 134.2 %copy-start = (bf16[256,256]{1,0:T(8,128)(2,1)S(1)}, bf16[256,256]{1,0:T(8,128)(2,1)}, u32[]{:S(2)}) copy-start(bf16[256,256]{1,0:T(8,128)(2,1)} %param.9) | copy-start | bytes 393220
  0.0 11.8 %collective-permute-start = (bf16[256,512]{1,0:T(8,128)(2,1)}, bf16[256,512]{1,0:T(8,128)(2,1)S(1)}, u32[]{:S(2)}, u32[]{:S(2)}) collective-permute-start(bf16[256,512]{1,0:T(8,128)(2,1)} %param.8), channel_id=1, source_target_pairs={{0,128},{1,129},{32,160},{33,161},{64,192},{65,193},{96,224},{97,2... | collective-permute-start | bytes 786440 | tf_op jit(solution)/shard_map/ppermute | solution.py:330
  3.0 8.8 %collective-permute-start.1 = (bf16[256,512]{1,0:T(8,128)(2,1)}, bf16[256,512]{1,0:T(8,128)(2,1)S(1)}, u32[]{:S(2)}, u32[]{:S(2)}) collective-permute-start(bf16[256,512]{1,0:T(8,128)(2,1)} %param.8), channel_id=1, source_target_pairs={{0,32},{1,33},{32,0},{33,1},{64,96},{65,97},{96,64},{97,65},{128,1... | collective-permute-start | bytes 786440 | tf_op jit(solution)/shard_map/ppermute | solution.py:330
  4.6 16.9 %collective-permute-start.2 = (bf16[256,512]{1,0:T(8,128)(2,1)}, bf16[256,512]{1,0:T(8,128)(2,1)S(1)}, u32[]{:S(2)}, u32[]{:S(2)}) collective-permute-start(bf16[256,512]{1,0:T(8,128)(2,1)} %param.8), channel_id=1, source_target_pairs={{0,64},{1,65},{32,96},{33,97},{64,128},{65,129},{96,160},{97,161},... | collective-permute-start | bytes 786440 | tf_op jit(solution)/shard_map/ppermute | solution.py:330
  5.2 16.3 %collective-permute-start.3 = (bf16[256,512]{1,0:T(8,128)(2,1)}, bf16[256,512]{1,0:T(8,128)(2,1)S(1)}, u32[]{:S(2)}, u32[]{:S(2)}) collective-permute-start(bf16[256,512]{1,0:T(8,128)(2,1)} %param.8), channel_id=1, source_target_pairs={{0,192},{1,193},{32,224},{33,225},{64,0},{65,1},{96,32},{97,33},{1... | collective-permute-start | bytes 786440 | tf_op jit(solution)/shard_map/ppermute | solution.py:330
  7.8 9.5 %copy-start.2 = (bf16[256,512]{1,0:T(8,128)(2,1)S(1)}, bf16[256,512]{1,0:T(8,128)(2,1)}, u32[]{:S(2)}) copy-start(bf16[256,512]{1,0:T(8,128)(2,1)} %param.8) | copy-start | bytes 786436
  11.9 9.6 %collective-permute-start.4 = (bf16[256,512]{1,0:T(8,128)(2,1)S(1)}, bf16[256,512]{1,0:T(8,128)(2,1)S(1)}, u32[]{:S(2)}, u32[]{:S(2)}) collective-permute-start(bf16[256,512]{1,0:T(8,128)(2,1)S(1)} %get-tuple-element.33.refs_1_), channel_id=1, source_target_pairs={{0,64},{1,65},{32,96},{33,97},{64,128},{65,129},{96,160},{97,161},... | collective-permute-start | bytes 786440 | tf_op jit(solution)/shard_map/ppermute | solution.py:330
  12.5 9.1 %collective-permute-start.5 = (bf16[256,512]{1,0:T(8,128)(2,1)S(1)}, bf16[256,512]{1,0:T(8,128)(2,1)S(1)}, u32[]{:S(2)}, u32[]{:S(2)}) collective-permute-start(bf16[256,512]{1,0:T(8,128)(2,1)S(1)} %get-tuple-element.33.refs_1_), channel_id=1, source_target_pairs={{0,192},{1,193},{32,224},{33,225},{64,0},{65,1},{96,32},{97,33},{1... | collective-permute-start | bytes 786440 | tf_op jit(solution)/shard_map/ppermute | solution.py:330
  15.2 7.6 %collective-permute-start.6 = (bf16[256,512]{1,0:T(8,128)(2,1)S(1)}, bf16[256,512]{1,0:T(8,128)(2,1)S(1)}, u32[]{:S(2)}, u32[]{:S(2)}) collective-permute-start(bf16[256,512]{1,0:T(8,128)(2,1)S(1)} %get-tuple-element.35.refs_4_), channel_id=1, source_target_pairs={{0,33},{1,32},{32,1},{33,0},{64,97},{65,96},{96,65},{97,64},{128,1... | collective-permute-start | bytes 786440 | tf_op jit(solution)/shard_map/ppermute | solution.py:330
  22.8 1.5 %collective-permute-start.10 = (bf16[256,512]{1,0:T(8,128)(2,1)S(1)}, bf16[256,512]{1,0:T(8,128)(2,1)S(1)}, u32[]{:S(2)}, u32[]{:S(2)}) collective-permute-start(bf16[256,512]{1,0:T(8,128)(2,1)S(1)} %get-tuple-element.40.refs_5_.refs_3_), channel_id=1, source_target_pairs={{0,16},{16,0},{1,17},{17,1},{2,18},{18,2},{3,19},{19,3},{4,20},{20... | collective-permute-start | bytes 786440 | tf_op jit(solution)/shard_map/ppermute | solution.py:299
  22.8 1.9 %collective-permute-start.11 = (bf16[256,512]{1,0:T(8,128)(2,1)S(1)}, bf16[256,512]{1,0:T(8,128)(2,1)S(1)}, u32[]{:S(2)}, u32[]{:S(2)}) collective-permute-start(bf16[256,512]{1,0:T(8,128)(2,1)S(1)} %get-tuple-element.41.refs_6_.refs_4_), channel_id=1, source_target_pairs={{0,16},{16,0},{1,17},{17,1},{2,18},{18,2},{3,19},{19,3},{4,20},{20... | collective-permute-start | bytes 786440 | tf_op jit(solution)/shard_map/ppermute | solution.py:299
  23.3 1.8 %collective-permute-start.7 = (bf16[256,512]{1,0:T(8,128)(2,1)S(1)}, bf16[256,512]{1,0:T(8,128)(2,1)S(1)}, u32[]{:S(2)}, u32[]{:S(2)}) collective-permute-start(bf16[256,512]{1,0:T(8,128)(2,1)S(1)} %get-tuple-element.37.refs_2_.refs_0_), channel_id=1, source_target_pairs={{0,16},{16,0},{1,17},{17,1},{2,18},{18,2},{3,19},{19,3},{4,20},{20... | collective-permute-start | bytes 786440 | tf_op jit(solution)/shard_map/ppermute | solution.py:299
  23.3 2.1 %collective-permute-start.8 = (bf16[256,512]{1,0:T(8,128)(2,1)S(1)}, bf16[256,512]{1,0:T(8,128)(2,1)S(1)}, u32[]{:S(2)}, u32[]{:S(2)}) collective-permute-start(bf16[256,512]{1,0:T(8,128)(2,1)S(1)} %get-tuple-element.38.refs_3_.refs_1_), channel_id=1, source_target_pairs={{0,16},{16,0},{1,17},{17,1},{2,18},{18,2},{3,19},{19,3},{4,20},{20... | collective-permute-start | bytes 786440 | tf_op jit(solution)/shard_map/ppermute | solution.py:299
  23.8 2.0 %collective-permute-start.9 = (bf16[256,512]{1,0:T(8,128)(2,1)S(1)}, bf16[256,512]{1,0:T(8,128)(2,1)S(1)}, u32[]{:S(2)}, u32[]{:S(2)}) collective-permute-start(bf16[256,512]{1,0:T(8,128)(2,1)S(1)} %get-tuple-element.39.refs_4_.refs_2_), channel_id=1, source_target_pairs={{0,16},{16,0},{1,17},{17,1},{2,18},{18,2},{3,19},{19,3},{4,20},{20... | collective-permute-start | bytes 786440 | tf_op jit(solution)/shard_map/ppermute | solution.py:299
  24.3 1.9 %collective-permute-start.12 = (bf16[256,512]{1,0:T(8,128)(2,1)S(1)}, bf16[256,512]{1,0:T(8,128)(2,1)S(1)}, u32[]{:S(2)}, u32[]{:S(2)}) collective-permute-start(bf16[256,512]{1,0:T(8,128)(2,1)S(1)} %collective-permute-done.4.refs_7_.refs_5_), channel_id=1, source_target_pairs={{0,16},{16,0},{1,17},{17,1},{2,18},{18,2},{3,19},{19,3},{4,20},{20... | collective-permute-start | bytes 786440 | tf_op jit(solution)/shard_map/ppermute | solution.py:299
  24.7 1.9 %collective-permute-start.13 = (bf16[256,512]{1,0:T(8,128)(2,1)S(1)}, bf16[256,512]{1,0:T(8,128)(2,1)S(1)}, u32[]{:S(2)}, u32[]{:S(2)}) collective-permute-start(bf16[256,512]{1,0:T(8,128)(2,1)S(1)} %collective-permute-done.5.refs_8_.refs_6_), channel_id=1, source_target_pairs={{0,16},{16,0},{1,17},{17,1},{2,18},{18,2},{3,19},{19,3},{4,20},{20... | collective-permute-start | bytes 786440 | tf_op jit(solution)/shard_map/ppermute | solution.py:299
  25.1 1.9 %collective-permute-start.14 = (bf16[256,512]{1,0:T(8,128)(2,1)S(1)}, bf16[256,512]{1,0:T(8,128)(2,1)S(1)}, u32[]{:S(2)}, u32[]{:S(2)}) collective-permute-start(bf16[256,512]{1,0:T(8,128)(2,1)S(1)} %collective-permute-done.6.refs_9_.refs_7_), channel_id=1, source_target_pairs={{0,16},{16,0},{1,17},{17,1},{2,18},{18,2},{3,19},{19,3},{4,20},{20... | collective-permute-start | bytes 786440 | tf_op jit(solution)/shard_map/ppermute | solution.py:299
  27.9 7.5 %collective-permute-start.15 = (f32[16,512]{1,0:T(8,128)S(1)}, f32[16,512]{1,0:T(8,128)S(1)}, u32[]{:S(2)}, u32[]{:S(2)}) collective-permute-start(f32[16,512]{1,0:T(8,128)S(1)} %get-tuple-element.50), channel_id=1, source_target_pairs={{0,1},{1,0},{2,3},{3,2},{4,5},{5,4},{6,7},{7,6},{8,9},{9,8},{10,11... | collective-permute-start | bytes 98312 | tf_op jit(solution)/shard_map/ppermute | solution.py:346
  29.7 5.7 %collective-permute-start.16 = (f32[16,512]{1,0:T(8,128)S(1)}, f32[16,512]{1,0:T(8,128)S(1)}, u32[]{:S(2)}, u32[]{:S(2)}) collective-permute-start(f32[16,512]{1,0:T(8,128)S(1)} %get-tuple-element.51), channel_id=1, source_target_pairs={{0,2},{1,3},{2,0},{3,1},{4,6},{5,7},{6,4},{7,5},{8,10},{9,11},{10,... | collective-permute-start | bytes 98312 | tf_op jit(solution)/shard_map/ppermute | solution.py:346
  29.8 6.3 %collective-permute-start.17 = (f32[16,512]{1,0:T(8,128)S(1)}, f32[16,512]{1,0:T(8,128)S(1)}, u32[]{:S(2)}, u32[]{:S(2)}) collective-permute-start(f32[16,512]{1,0:T(8,128)S(1)} %get-tuple-element.52), channel_id=1, source_target_pairs={{0,3},{1,2},{2,1},{3,0},{4,7},{5,6},{6,5},{7,4},{8,11},{9,10},{10,... | collective-permute-start | bytes 98312 | tf_op jit(solution)/shard_map/ppermute | solution.py:346
  33.0 11.9 %copy-start.1 = (f32[1,1024]{1,0:T(1,128)S(1)}, f32[1,1024]{1,0:T(1,128)}, u32[]{:S(2)}) copy-start(f32[1,1024]{1,0:T(1,128)} %scale_ref.1) | copy-start | bytes 12292
  36.2 11.3 %collective-permute-start.18 = (f32[16,512]{1,0:T(8,128)S(1)}, f32[16,512]{1,0:T(8,128)S(1)}, u32[]{:S(2)}, u32[]{:S(2)}) collective-permute-start(f32[16,512]{1,0:T(8,128)S(1)} %add_add_fusion.1), channel_id=1, source_target_pairs={{0,4},{1,5},{2,6},{3,7},{4,0},{5,1},{6,2},{7,3},{8,12},{9,13},{10,... | collective-permute-start | bytes 98312 | tf_op jit(solution)/shard_map/ppermute | solution.py:346
  39.5 8.1 %collective-permute-start.19 = (f32[16,512]{1,0:T(8,128)S(1)}, f32[16,512]{1,0:T(8,128)S(1)}, u32[]{:S(2)}, u32[]{:S(2)}) collective-permute-start(f32[16,512]{1,0:T(8,128)S(1)} %add_add_fusion.1), channel_id=1, source_target_pairs={{0,8},{1,9},{2,10},{3,11},{4,12},{5,13},{6,14},{7,15},{8,0},{9,1},... | collective-permute-start | bytes 98312 | tf_op jit(solution)/shard_map/ppermute | solution.py:346
  44.9 6.0 %collective-permute-start.20 = (f32[16,512]{1,0:T(8,128)S(1)}, f32[16,512]{1,0:T(8,128)S(1)}, u32[]{:S(2)}, u32[]{:S(2)}) collective-permute-start(f32[16,512]{1,0:T(8,128)S(1)} %add_add_fusion.1), channel_id=1, source_target_pairs={{0,12},{1,13},{2,14},{3,15},{4,8},{5,9},{6,10},{7,11},{8,4},{9,5},... | collective-permute-start | bytes 98312 | tf_op jit(solution)/shard_map/ppermute | solution.py:346
  51.0 5.5 %collective-permute-start.21 = (f32[16,512]{1,0:T(8,128)S(1)}, f32[16,512]{1,0:T(8,128)S(1)}, u32[]{:S(2)}, u32[]{:S(2)}) collective-permute-start(f32[16,512]{1,0:T(8,128)S(1)} %add_add_fusion.refs_4_), channel_id=1, source_target_pairs={{0,1},{1,0},{2,3},{3,2},{4,5},{5,4},{6,7},{7,6},{8,9},{9,8},{10,11... | collective-permute-start | bytes 98312 | tf_op jit(solution)/shard_map/ppermute | solution.py:346
  52.9 3.9 %collective-permute-start.22 = (f32[16,512]{1,0:T(8,128)S(1)}, f32[16,512]{1,0:T(8,128)S(1)}, u32[]{:S(2)}, u32[]{:S(2)}) collective-permute-start(f32[16,512]{1,0:T(8,128)S(1)} %add_add_fusion.refs_4_), channel_id=1, source_target_pairs={{0,2},{1,3},{2,0},{3,1},{4,6},{5,7},{6,4},{7,5},{8,10},{9,11},{10,... | collective-permute-start | bytes 98312 | tf_op jit(solution)/shard_map/ppermute | solution.py:346
  53.9 6.3 %collective-permute-start.23 = (f32[16,512]{1,0:T(8,128)S(1)}, f32[16,512]{1,0:T(8,128)S(1)}, u32[]{:S(2)}, u32[]{:S(2)}) collective-permute-start(f32[16,512]{1,0:T(8,128)S(1)} %add_add_fusion.refs_4_), channel_id=1, source_target_pairs={{0,3},{1,2},{2,1},{3,0},{4,7},{5,6},{6,5},{7,4},{8,11},{9,10},{10,... | collective-permute-start | bytes 98312 | tf_op jit(solution)/shard_map/ppermute | solution.py:346
  61.8 2.7 %collective-permute-start.25 = (bf16[4,512,256]{2,1,0:T(8,128)(2,1)S(1)}, bf16[4,512,256]{2,1,0:T(8,128)(2,1)S(1)}, u32[]{:S(2)}, u32[]{:S(2)}) collective-permute-start(bf16[4,512,256]{2,1,0:T(8,128)(2,1)S(1)} %get-tuple-element.56), channel_id=1, source_target_pairs={{0,16},{16,0},{1,17},{17,1},{2,18},{18,2},{3,19},{19,3},{4,20},{20... | collective-permute-start | bytes 3145736 | tf_op jit(solution)/shard_map/ppermute | solution.py:299
  63.2 2.9 %collective-permute-start.24 = (bf16[4,512,256]{2,1,0:T(8,128)(2,1)S(1)}, bf16[4,512,256]{2,1,0:T(8,128)(2,1)S(1)}, u32[]{:S(2)}, u32[]{:S(2)}) collective-permute-start(bf16[4,512,256]{2,1,0:T(8,128)(2,1)S(1)} %back.1), channel_id=1, source_target_pairs={{0,16},{16,0},{1,17},{17,1},{2,18},{18,2},{3,19},{19,3},{4,20},{20... | collective-permute-start | bytes 3145736 | tf_op jit(solution)/shard_map/ppermute | solution.py:299
where the time goes:
time: 135 us
  blocking collectives  66.2 us (49%)
  starting transfers between devices  34.3 us (25%)
  Pallas kernels  19.5 us (14%)
  waiting for transfers between devices  13.3 us (10%)
    all_to_all x3, blocking collectives, exchange(): return lax.all_to_all(value, axes, 0, 0, tiled=True)  66.2 us
    ppermute x9, starting transfers between devices, trade(): received.append(lax.ppermute(value, ('z', 'yh'), pairs))  18.9 us
    ppermute x7, starting transfers between devices, shift(): return lax.ppermute(value, ('x', 'yl', 'yh'), pairs)  13.3 us
    pallas_call x7, Pallas kernels, inside(): pl.pallas_call(kernel, out_shape=out_shape, in_specs=[INSIDE] * len(opera...  11.4 us
    ppermute x9, waiting for transfers between devices, trade(): received.append(lax.ppermute(value, ('z', 'yh'), pairs))  8.34 us
    pallas_call x2, Pallas kernels, mask(): pl.pallas_call(functools.partial(mask_kernel, tile=tile, last=last), out_...  8.1 us
    ppermute x10, waiting for transfers between devices, swap(): return lax.ppermute(value, 'c', [(0, 1), (1, 0)])  3.72 us
  transfers between devices with their start and end apart: 26, of which 17 were waited for; matrix products, arithmetic and copies ran while one was open for 0% of the time, Pallas kernels for 12%

commit v1 on v0

--- a/solution.py
+++ b/solution.py
@@ -75,7 +75,7 @@
 
 
 def member():
-    return lax.rem(lax.axis_index("z"), 2) * 2 + lax.axis_index("yh")
+    return lax.axis_index("zl") * 2 + lax.axis_index("yh")
 
 
 def portion_rows(change, count):
@@ -124,11 +124,9 @@
     return jnp.dot(solved_ref[...], masked, preferred_element_type=F32)
 
 
-def solve_back_kernel(scaled_ref, *refs):
-    left_refs, masked_refs, part_refs = refs[:TILES], refs[TILES : 2 * TILES], refs[2 * TILES : -3]
-    solved_ref, out_ref, projection_ref = refs[-3:]
-    for change, part_ref in enumerate(part_refs):
-        projection_ref[portion_rows(change, part_ref.shape[0]), :] = part_ref[...]
+def solve_back_kernel(scaled_ref, projection_ref, *refs):
+    left_refs, masked_refs = refs[:TILES], refs[TILES : 2 * TILES]
+    solved_ref, out_ref = refs[-2:]
     pieces = jnp.concatenate(split3(projection_ref[...]), axis=0)
     for tile, left_ref in enumerate(left_refs):
         low_rank = lax.dot_general(
@@ -260,15 +258,15 @@
     )
 
 
-def solve_back(scaled, parts, left, masked, count):
+def solve_back(scaled, projection, left, masked, count):
     vectors, rows = scaled.shape
     out = (
         jax.ShapeDtypeStruct((vectors, rows), BF16),
         jax.ShapeDtypeStruct((count, vectors, BLOCK), BF16),
     )
     return inside(
-        solve_back_kernel, "solve_back", out, (scaled, *left, *masked, *parts),
-        2 * rows * count * BLOCK * vectors, None, [pltpu.VMEM((RANK, vectors), F32)],
+        solve_back_kernel, "solve_back", out, (scaled, projection, *left, *masked),
+        2 * rows * count * BLOCK * vectors,
     )
 
 
@@ -330,12 +328,13 @@
     return lax.ppermute(value, ("x", "yl", "yh"), pairs)
 
 
+LAYERS = ("zh", "zl")
 NEAR = ((0, 1), (1, 0), (1, 1))
-APART = ((2, 0), (4, 0), (6, 0))
+APART = ((4, 0), (2, 0), (6, 0))
 
 
 def trade(values, partners):
-    layers, halves = lax.axis_size("z"), lax.axis_size("yh")
+    layers, halves = lax.axis_size(LAYERS), lax.axis_size("yh")
     received = []
     for value, (dz, dh) in zip(values, partners):
         pairs = [
@@ -343,7 +342,7 @@
             for z in range(layers)
             for h in range(halves)
         ]
-        received.append(lax.ppermute(value, ("z", "yh"), pairs))
+        received.append(lax.ppermute(value, (*LAYERS, "yh"), pairs))
     return received
 
 
@@ -361,7 +360,7 @@
     basis_right,
     interior_scale,
 ):
-    members = lax.axis_size("z") * lax.axis_size("yh")
+    members = lax.axis_size((*LAYERS, "yh"))
     block_rows, vectors = interface_panel.shape
     here = interface_panel
     across, beside = shift(here, 2, 0), shift(here, 0, 1)
@@ -382,30 +381,30 @@
     scaled, token_2 = load_second(other, theirs, first, interior_scale)
     keep = total(keep, received, token_1)
     keep = total(keep, trade([keep] * 3, APART), token_2)
-    parts = [keep] + trade([keep] * 3, NEAR)
+    parts = jnp.broadcast_to(keep[None], (4,) + keep.shape)
+    projection = exchange(parts, ("zl", "yh")).reshape(RANK, vectors)
 
     half = len(STEPS) // 2
-    solved, give = solve_back(scaled, parts, left, other, half)
+    solved, give = solve_back(scaled, projection, left, other, half)
     give_1 = swap(give)
     give_2 = swap(back(solved, other, half, half))
     term = back_add(solved, own, 0, give_1, ())
     term = back_add(solved, own, half, give_2, (term,))
 
-    halves, layers = lax.axis_size("yh"), lax.axis_size("z")
+    halves, layers = lax.axis_size("yh"), lax.axis_size(LAYERS)
     part, piece = vectors // halves, vectors // members
     term = term.reshape(len(STEPS) * halves, part, block_rows)
     term = jnp.sum(exchange(term, ("x", "yl", "yh")).astype(F32), axis=0)
-    term = jnp.sum(exchange(term.reshape(layers, piece, block_rows), "z"), axis=0)
-    term = exchange(jnp.broadcast_to(term[None], (members, piece, block_rows)), ("yh", "z"))
+    term = jnp.sum(exchange(term.reshape(layers, piece, block_rows), LAYERS), axis=0)
+    term = exchange(jnp.broadcast_to(term[None], (members, piece, block_rows)), ("yh", *LAYERS))
     coupled = term.reshape(vectors, block_rows).T
     local_image = jnp.dot(interface_block, interface_panel, preferred_element_type=F32)
     return local_image - coupled
 
 
 def solution(mesh):
-    shape = (4, 2, 2, 8, 2)
-    fine = jax.sharding.Mesh(mesh.devices.reshape(shape), ("x", "yl", "c", "z", "yh"))
-    dom, grp = ("x", "yl", "c"), ("z", "yh")
+    dom, grp = ("x", "yl", "c"), ("zh", "zl", "yh")
+    fine = jax.sharding.Mesh(mesh.devices.reshape(4, 2, 2, 4, 2, 2), dom + grp)
     return jax.shard_map(
         local,
         mesh=fine,

time: 135 us -> 134 us (level)
  blocking collectives: 66.2 us -> 74.1 us
  starting transfers between devices: 34.3 us -> 29.2 us
  waiting for transfers between devices: 13.3 us -> 9.16 us
    all_to_all x3 -> x4, blocking collectives: 66.2 us -> 74.1 us  [exchange(): return lax.all_to_all(value, axes, 0, 0, tiled=True)]
    ppermute x9 -> x6, starting transfers between devices: 18.9 us -> 13.8 us  [trade(): received.append(lax.ppermute(value, (*LAYERS, 'yh'), pairs))]
    ppermute x9 -> x6, waiting for transfers between devices: 8.34 us -> 4.16 us  [trade(): received.append(lax.ppermute(value, (*LAYERS, 'yh'), pairs))]
  transfers between devices with their start and end apart: 26 -> 23, of which waited for: 17 -> 14; matrix products, arithmetic and copies ran while one was open for 0% -> 0% of each run, Pallas kernels for 12% -> 12%
where the time goes in v1:
time: 134 us
  blocking collectives  74.1 us (55%)
  starting transfers between devices  29.2 us (22%)
  Pallas kernels  19.4 us (14%)
  waiting for transfers between devices  9.16 us (7%)
    all_to_all x4, blocking collectives, exchange(): return lax.all_to_all(value, axes, 0, 0, tiled=True)  74.1 us
    ppermute x6, starting transfers between devices, trade(): received.append(lax.ppermute(value, (*LAYERS, 'yh'), pairs))  13.8 us
    ppermute x7, starting transfers between devices, shift(): return lax.ppermute(value, ('x', 'yl', 'yh'), pairs)  13.3 us
    pallas_call x7, Pallas kernels, inside(): pl.pallas_call(kernel, out_shape=out_shape, in_specs=[INSIDE] * len(opera...  11.3 us
    pallas_call x2, Pallas kernels, mask(): pl.pallas_call(functools.partial(mask_kernel, tile=tile, last=last), out_...  8.1 us
    ppermute x6, waiting for transfers between devices, trade(): received.append(lax.ppermute(value, (*LAYERS, 'yh'), pairs))  4.16 us
    ppermute x10, waiting for transfers between devices, swap(): return lax.ppermute(value, 'c', [(0, 1), (1, 0)])  3.72 us
  transfers between devices with their start and end apart: 23, of which 14 were waited for; matrix products, arithmetic and copies ran while one was open for 0% of the time, Pallas kernels for 12%

profile of v1, /device:TPU:32, one launch (start us, length us, event | category | flops | bytes accessed | tf_op | source)
XLA Modules:
  0.0 133.8 jit_solution(5650916619935397254)
XLA Ops:
  0.0 0.0 copy-start
  0.0 3.0 %collective-permute-start = (bf16[256,512]{1,0:T(8,128)(2,1)}, bf16[256,512]{1,0:T(8,128)(2,1)S(1)}, u32[]{:S(2)}, u32[]{:S(2)}) collective-permute-start(bf16[256,512]{1,0:T(8,128)(2,1)} %param.8), channel_id=1, source_target_pairs={{0,128},{1,129},{32,160},{33,161},{64,192},{65,193},{96,224},{97,2... | collective-permute-start | bytes 786440 | tf_op jit(solution)/shard_map/ppermute | solution.py:328
  3.0 1.6 %collective-permute-start.1 = (bf16[256,512]{1,0:T(8,128)(2,1)}, bf16[256,512]{1,0:T(8,128)(2,1)S(1)}, u32[]{:S(2)}, u32[]{:S(2)}) collective-permute-start(bf16[256,512]{1,0:T(8,128)(2,1)} %param.8), channel_id=1, source_target_pairs={{0,32},{1,33},{32,0},{33,1},{64,96},{65,97},{96,64},{97,65},{128,1... | collective-permute-start | bytes 786440 | tf_op jit(solution)/shard_map/ppermute | solution.py:328
  4.6 0.6 collective-permute-start.2
  5.2 2.6 %collective-permute-start.3 = (bf16[256,512]{1,0:T(8,128)(2,1)}, bf16[256,512]{1,0:T(8,128)(2,1)S(1)}, u32[]{:S(2)}, u32[]{:S(2)}) collective-permute-start(bf16[256,512]{1,0:T(8,128)(2,1)} %param.8), channel_id=1, source_target_pairs={{0,192},{1,193},{32,224},{33,225},{64,0},{65,1},{96,32},{97,33},{1... | collective-permute-start | bytes 786440 | tf_op jit(solution)/shard_map/ppermute | solution.py:328
  7.8 4.0 %mask.2 = (bf16[512,2048]{1,0:T(8,128)(2,1)S(1)}, bf16[512,2048]{1,0:T(8,128)(2,1)S(1)}, bf16[192,512]{1,0:T(8,128)(2,1)S(1)}, f32[2,64,2048]{2,1,0:T(8,128)S(1)}) custom-call(s32[2,16]{1,0:T(2,128)} %bitcast.23, s32[2]{0:T(128)} %bitcast.25, bf16[1024,4096]{1,0:T(8,128)(2,1)} %bitcast.15, bf16[64,1024]{1,0:T(8,128)(2,1)} %bitcast.19, bf16[64,1024]{1,0:T(8,128)(2,1)} %bitcast.21), custom_call_target="tpu_custom_call" | custom-call | flops 268435456 | bytes 8388608 | tf_op jit(solution)/shard_map/mask/pallas_call | solution.py:192
  11.8 0.0 collective-permute-done.refs_0_
  11.9 0.0 collective-permute-done.1.refs_1_
  11.9 0.6 collective-permute-start.4
  12.5 2.7 %collective-permute-start.5 = (bf16[256,512]{1,0:T(8,128)(2,1)S(1)}, bf16[256,512]{1,0:T(8,128)(2,1)S(1)}, u32[]{:S(2)}, u32[]{:S(2)}) collective-permute-start(bf16[256,512]{1,0:T(8,128)(2,1)S(1)} %get-tuple-element.33.refs_1_), channel_id=1, source_target_pairs={{0,192},{1,193},{32,224},{33,225},{64,0},{65,1},{96,32},{97,33},{1... | collective-permute-start | bytes 786440 | tf_op jit(solution)/shard_map/ppermute | solution.py:328
  15.2 2.1 %collective-permute-start.6 = (bf16[256,512]{1,0:T(8,128)(2,1)S(1)}, bf16[256,512]{1,0:T(8,128)(2,1)S(1)}, u32[]{:S(2)}, u32[]{:S(2)}) collective-permute-start(bf16[256,512]{1,0:T(8,128)(2,1)S(1)} %get-tuple-element.35.refs_4_), channel_id=1, source_target_pairs={{0,33},{1,32},{32,1},{33,0},{64,97},{65,96},{96,65},{97,64},{128,1... | collective-permute-start | bytes 786440 | tf_op jit(solution)/shard_map/ppermute | solution.py:328
  17.4 4.1 %mask.3 = (bf16[512,2048]{1,0:T(8,128)(2,1)S(1)}, bf16[512,2048]{1,0:T(8,128)(2,1)S(1)}, bf16[192,512]{1,0:T(8,128)(2,1)S(1)}, bf16[192,2048]{1,0:T(8,128)(2,1)S(1)}, bf16[192,2048]{1,0:T(8,128)(2,1)S(1)}) custom-call(s32[2,16]{1,0:T(2,128)} %bitcast.24, s32[2]{0:T(128)} %bitcast.26, bf16[1024,4096]{1,0:T(8,128)(2,1)} %bitcast.16, ...), custom_call_target="tpu_custom_call" | custom-call | flops 268435456 | bytes 8388608 | tf_op jit(solution)/shard_map/mask/pallas_call | solution.py:192
  21.5 0.0 collective-permute-done.2.refs_2_
  21.5 0.0 collective-permute-done.3.refs_3_
  21.5 0.0 collective-permute-done.4.refs_7_.refs_5_
  21.5 0.0 collective-permute-done.5.refs_8_.refs_6_
  21.5 1.3 collective-permute-done.6.refs_9_.refs_7_
  22.8 0.0 collective-permute-start.10
  22.8 0.5 collective-permute-start.11
  23.3 0.0 collective-permute-start.7
  23.3 0.5 collective-permute-start.8
  23.8 0.0 collective-permute-start.9
  23.8 0.5 collective-permute-done.10.refs_5_.refs_11_
  24.3 0.1 collective-permute-start.12
  24.5 0.2 collective-permute-done.11.refs_6_.refs_12_
  24.7 0.1 collective-permute-start.13
  24.8 0.2 collective-permute-done.7.refs_2_.refs_8_
  25.1 0.1 collective-permute-start.14
  25.2 0.2 collective-permute-done.8.refs_3_.refs_9_
  25.4 0.4 collective-permute-done.9.refs_4_.refs_10_
  25.8 0.4 collective-permute-done.12.refs_7_.refs_13_
  26.2 0.4 collective-permute-done.13.refs_8_.refs_14_
  26.6 0.4 collective-permute-done.14.refs_9_.refs_15_
  26.9 1.0 project.1
  27.9 1.8 %collective-permute-start.15 = (f32[16,512]{1,0:T(8,128)S(1)}, f32[16,512]{1,0:T(8,128)S(1)}, u32[]{:S(2)}, u32[]{:S(2)}) collective-permute-start(f32[16,512]{1,0:T(8,128)S(1)} %get-tuple-element.49), channel_id=1, source_target_pairs={{0,1},{1,0},{2,3},{3,2},{4,5},{5,4},{6,7},{7,6},{8,9},{9,8},{10,11... | collective-permute-start | bytes 98312 | tf_op jit(solution)/shard_map/ppermute | solution.py:345
  29.7 0.1 collective-permute-start.16
  29.8 3.2 %collective-permute-start.17 = (f32[16,512]{1,0:T(8,128)S(1)}, f32[16,512]{1,0:T(8,128)S(1)}, u32[]{:S(2)}, u32[]{:S(2)}) collective-permute-start(f32[16,512]{1,0:T(8,128)S(1)} %get-tuple-element.51), channel_id=1, source_target_pairs={{0,3},{1,2},{2,1},{3,0},{4,7},{5,6},{6,5},{7,4},{8,11},{9,10},{10,... | collective-permute-start | bytes 98312 | tf_op jit(solution)/shard_map/ppermute | solution.py:345
  33.0 2.4 %load_first.1 = (f32[1024,512]{1,0:T(8,128)S(1)}, f32[16,512]{1,0:T(8,128)S(1)}) custom-call(bf16[512,2048]{1,0:T(8,128)(2,1)S(1)} %get-tuple-element.31.refs_0_, bf16[512,2048]{1,0:T(8,128)(2,1)S(1)} %get-tuple-element.34.refs_1_, bf16[256,512]{1,0:T(8,128)(2,1)S(1)} %get-tuple-element.37.refs_2_.refs_0_, ...), custom_call_target="tpu_custom_call" | custom-call | flops 2147483648 | bytes 1048576 | tf_op jit(solution)/shard_map/load_first/pallas_call | solution.py:217
  35.4 0.0 collective-permute-done.15
  35.4 0.0 collective-permute-done.16
  35.4 0.7 collective-permute-done.17
  36.2 7.3 %collective-permute-start.18 = (f32[16,512]{1,0:T(8,128)S(1)}, f32[16,512]{1,0:T(8,128)S(1)}, u32[]{:S(2)}, u32[]{:S(2)}) collective-permute-start(f32[16,512]{1,0:T(8,128)S(1)} %add_add_fusion.1), channel_id=1, source_target_pairs={{0,8},{1,9},{2,10},{3,11},{4,12},{5,13},{6,14},{7,15},{8,0},{9,1},... | collective-permute-start | bytes 98312 | tf_op jit(solution)/shard_map/ppermute | solution.py:345
  43.4 1.5 %collective-permute-start.19 = (f32[16,512]{1,0:T(8,128)S(1)}, f32[16,512]{1,0:T(8,128)S(1)}, u32[]{:S(2)}, u32[]{:S(2)}) collective-permute-start(f32[16,512]{1,0:T(8,128)S(1)} %add_add_fusion.1), channel_id=1, source_target_pairs={{0,4},{1,5},{2,6},{3,7},{4,0},{5,1},{6,2},{7,3},{8,12},{9,13},{10,... | collective-permute-start | bytes 98312 | tf_op jit(solution)/shard_map/ppermute | solution.py:345
  44.9 0.0 collective-permute-start.20
  44.9 0.0 copy-done.1
  44.9 2.6 %load_second.1 = (f32[512,1024]{1,0:T(8,128)S(1)}, f32[16,512]{1,0:T(8,128)S(1)}) custom-call(f32[1024,512]{1,0:T(8,128)S(1)} %get-tuple-element.42.first_ref, f32[1,1024]{1,0:T(1,128)S(1)} %copy-done.1, bf16[512,2048]{1,0:T(8,128)(2,1)S(1)} %get-tuple-element.43.refs_0_.refs_2_, bf16[512,2048]{1,0:T(8,128)(2,1)S(1)} %get-tuple-element.44.refs_1_.refs_3_, ...), custom_call_target="tpu_custom_call" | custom-call | flops 2147483648 | bytes 1048576 | tf_op jit(solution)/shard_map/load_second/pallas_call | solution.py:217
  47.5 0.0 collective-permute-done.18
  47.5 1.1 collective-permute-done.19
  48.6 2.3 %collective-permute-done.20 = f32[16,512]{1,0:T(8,128)S(1)} collective-permute-done((f32[16,512]{1,0:T(8,128)S(1)}, f32[16,512]{1,0:T(8,128)S(1)}, u32[]{:S(2)}, u32[]{:S(2)}) %collective-permute-start.20) | collective-permute-done | bytes 32800 | tf_op jit(solution)/shard_map/ppermute | solution.py:345
  51.0 9.8 %all_to_all.20 = f32[4,16,512]{2,1,0:T(8,128)S(1)} all-to-all(f32[4,16,512]{2,1,0:T(8,128)S(1)} %broadcast_in_dim.4), channel_id=1, replica_groups=mesh['x'=4,'yl'=2,'c'=2,'zh'=4,'zl'=2,'yh'=2] {'zl','yh'}, dimensions={0} | all-to-all | bytes 262144 | tf_op jit(solution)/shard_map/all_to_all | solution.py:293
  60.8 1.6 %solve_back.1 = (bf16[512,1024]{1,0:T(8,128)(2,1)S(1)}, bf16[4,512,256]{2,1,0:T(8,128)(2,1)S(1)}) custom-call(f32[512,1024]{1,0:T(8,128)S(1)} %get-tuple-element.45.scaled_ref, f32[64,512]{1,0:T(8,128)S(1)} %bitcast.14, bf16[192,512]{1,0:T(8,128)(2,1)S(1)} %get-tuple-element.54.refs_0_, bf16[192,512]{1,0:T(8,128)(2,1)S(1)} %get-tuple-element.36.refs_5_.refs_1_, ...), custom_call_target="tpu_custom_call" | custom-call | flops 1073741824 | bytes 1048576 | tf_op jit(solution)/shard_map/solve_back/pallas_call | solution.py:217
  62.3 0.1 collective-permute-start.22
  62.4 1.2 back.1
  63.7 0.6 collective-permute-start.21
  64.3 0.8 collective-permute-done.22.refs_2_
  65.1 1.3 back_add.2.refs_3_
  66.4 0.2 collective-permute-done.21.refs_2_
  66.6 1.3 back_add.3
  67.9 32.0 %all_to_all.21 = bf16[16,256,256]{2,1,0:T(8,128)(2,1)S(1)} all-to-all(bf16[16,256,256]{2,1,0:T(8,128)(2,1)S(1)} %bitcast.13), channel_id=1, replica_groups=mesh['x'=4,'yl'=2,'c'=2,'zh'=4,'zl'=2,'yh'=2] {'x','yl','yh'}, dimensions={0} | all-to-all | bytes 4194304 | tf_op jit(solution)/shard_map/all_to_all | solution.py:293
  99.9 0.3 convert_reduce_fusion
  100.1 13.8 %all_to_all.22 = f32[8,32,256]{2,1,0:T(8,128)S(1)} all-to-all(f32[8,32,256]{2,1,0:T(8,128)S(1)} %bitcast.18), channel_id=1, replica_groups=mesh['x'=4,'yl'=2,'c'=2,'zh'=4,'zl'=2,'yh'=2] {'zh','zl'}, dimensions={0} | all-to-all | bytes 524288 | tf_op jit(solution)/shard_map/all_to_all | solution.py:293
  114.0 18.6 %all_to_all.23 = f32[16,32,256]{2,1,0:T(8,128)S(1)} all-to-all(f32[16,32,256]{2,1,0:T(8,128)S(1)} %broadcast_in_dim.5), channel_id=1, replica_groups=mesh['x'=4,'yl'=2,'c'=2,'zh'=4,'zl'=2,'yh'=2] {'yh','zh','zl'}, dimensions={0} | all-to-all | bytes 1048576 | tf_op jit(solution)/shard_map/all_to_all | solution.py:293
  132.6 0.2 copy.18
  132.8 1.0 convolution_subtract_fusion
  (12 shorter events, 0.1 us)
Async XLA Ops:
  0.0 132.8 %copy-start = (bf16[256,256]{1,0:T(8,128)(2,1)S(1)}, bf16[256,256]{1,0:T(8,128)(2,1)}, u32[]{:S(2)}) copy-start(bf16[256,256]{1,0:T(8,128)(2,1)} %param.9) | copy-start | bytes 393220
  0.0 11.8 %collective-permute-start = (bf16[256,512]{1,0:T(8,128)(2,1)}, bf16[256,512]{1,0:T(8,128)(2,1)S(1)}, u32[]{:S(2)}, u32[]{:S(2)}) collective-permute-start(bf16[256,512]{1,0:T(8,128)(2,1)} %param.8), channel_id=1, source_target_pairs={{0,128},{1,129},{32,160},{33,161},{64,192},{65,193},{96,224},{97,2... | collective-permute-start | bytes 786440 | tf_op jit(solution)/shard_map/ppermute | solution.py:328
  3.0 8.8 %collective-permute-start.1 = (bf16[256,512]{1,0:T(8,128)(2,1)}, bf16[256,512]{1,0:T(8,128)(2,1)S(1)}, u32[]{:S(2)}, u32[]{:S(2)}) collective-permute-start(bf16[256,512]{1,0:T(8,128)(2,1)} %param.8), channel_id=1, source_target_pairs={{0,32},{1,33},{32,0},{33,1},{64,96},{65,97},{96,64},{97,65},{128,1... | collective-permute-start | bytes 786440 | tf_op jit(solution)/shard_map/ppermute | solution.py:328
  4.6 16.9 %collective-permute-start.2 = (bf16[256,512]{1,0:T(8,128)(2,1)}, bf16[256,512]{1,0:T(8,128)(2,1)S(1)}, u32[]{:S(2)}, u32[]{:S(2)}) collective-permute-start(bf16[256,512]{1,0:T(8,128)(2,1)} %param.8), channel_id=1, source_target_pairs={{0,64},{1,65},{32,96},{33,97},{64,128},{65,129},{96,160},{97,161},... | collective-permute-start | bytes 786440 | tf_op jit(solution)/shard_map/ppermute | solution.py:328
  5.2 16.3 %collective-permute-start.3 = (bf16[256,512]{1,0:T(8,128)(2,1)}, bf16[256,512]{1,0:T(8,128)(2,1)S(1)}, u32[]{:S(2)}, u32[]{:S(2)}) collective-permute-start(bf16[256,512]{1,0:T(8,128)(2,1)} %param.8), channel_id=1, source_target_pairs={{0,192},{1,193},{32,224},{33,225},{64,0},{65,1},{96,32},{97,33},{1... | collective-permute-start | bytes 786440 | tf_op jit(solution)/shard_map/ppermute | solution.py:328
  7.8 9.5 %copy-start.2 = (bf16[256,512]{1,0:T(8,128)(2,1)S(1)}, bf16[256,512]{1,0:T(8,128)(2,1)}, u32[]{:S(2)}) copy-start(bf16[256,512]{1,0:T(8,128)(2,1)} %param.8) | copy-start | bytes 786436
  11.9 9.6 %collective-permute-start.4 = (bf16[256,512]{1,0:T(8,128)(2,1)S(1)}, bf16[256,512]{1,0:T(8,128)(2,1)S(1)}, u32[]{:S(2)}, u32[]{:S(2)}) collective-permute-start(bf16[256,512]{1,0:T(8,128)(2,1)S(1)} %get-tuple-element.33.refs_1_), channel_id=1, source_target_pairs={{0,64},{1,65},{32,96},{33,97},{64,128},{65,129},{96,160},{97,161},... | collective-permute-start | bytes 786440 | tf_op jit(solution)/shard_map/ppermute | solution.py:328
  12.5 9.1 %collective-permute-start.5 = (bf16[256,512]{1,0:T(8,128)(2,1)S(1)}, bf16[256,512]{1,0:T(8,128)(2,1)S(1)}, u32[]{:S(2)}, u32[]{:S(2)}) collective-permute-start(bf16[256,512]{1,0:T(8,128)(2,1)S(1)} %get-tuple-element.33.refs_1_), channel_id=1, source_target_pairs={{0,192},{1,193},{32,224},{33,225},{64,0},{65,1},{96,32},{97,33},{1... | collective-permute-start | bytes 786440 | tf_op jit(solution)/shard_map/ppermute | solution.py:328
  15.2 7.6 %collective-permute-start.6 = (bf16[256,512]{1,0:T(8,128)(2,1)S(1)}, bf16[256,512]{1,0:T(8,128)(2,1)S(1)}, u32[]{:S(2)}, u32[]{:S(2)}) collective-permute-start(bf16[256,512]{1,0:T(8,128)(2,1)S(1)} %get-tuple-element.35.refs_4_), channel_id=1, source_target_pairs={{0,33},{1,32},{32,1},{33,0},{64,97},{65,96},{96,65},{97,64},{128,1... | collective-permute-start | bytes 786440 | tf_op jit(solution)/shard_map/ppermute | solution.py:328
  22.8 1.5 %collective-permute-start.10 = (bf16[256,512]{1,0:T(8,128)(2,1)S(1)}, bf16[256,512]{1,0:T(8,128)(2,1)S(1)}, u32[]{:S(2)}, u32[]{:S(2)}) collective-permute-start(bf16[256,512]{1,0:T(8,128)(2,1)S(1)} %get-tuple-element.40.refs_5_.refs_3_), channel_id=1, source_target_pairs={{0,16},{16,0},{1,17},{17,1},{2,18},{18,2},{3,19},{19,3},{4,20},{20... | collective-permute-start | bytes 786440 | tf_op jit(solution)/shard_map/ppermute | solution.py:297
  22.8 1.9 %collective-permute-start.11 = (bf16[256,512]{1,0:T(8,128)(2,1)S(1)}, bf16[256,512]{1,0:T(8,128)(2,1)S(1)}, u32[]{:S(2)}, u32[]{:S(2)}) collective-permute-start(bf16[256,512]{1,0:T(8,128)(2,1)S(1)} %get-tuple-element.41.refs_6_.refs_4_), channel_id=1, source_target_pairs={{0,16},{16,0},{1,17},{17,1},{2,18},{18,2},{3,19},{19,3},{4,20},{20... | collective-permute-start | bytes 786440 | tf_op jit(solution)/shard_map/ppermute | solution.py:297
  23.3 1.8 %collective-permute-start.7 = (bf16[256,512]{1,0:T(8,128)(2,1)S(1)}, bf16[256,512]{1,0:T(8,128)(2,1)S(1)}, u32[]{:S(2)}, u32[]{:S(2)}) collective-permute-start(bf16[256,512]{1,0:T(8,128)(2,1)S(1)} %get-tuple-element.37.refs_2_.refs_0_), channel_id=1, source_target_pairs={{0,16},{16,0},{1,17},{17,1},{2,18},{18,2},{3,19},{19,3},{4,20},{20... | collective-permute-start | bytes 786440 | tf_op jit(solution)/shard_map/ppermute | solution.py:297
  23.3 2.1 %collective-permute-start.8 = (bf16[256,512]{1,0:T(8,128)(2,1)S(1)}, bf16[256,512]{1,0:T(8,128)(2,1)S(1)}, u32[]{:S(2)}, u32[]{:S(2)}) collective-permute-start(bf16[256,512]{1,0:T(8,128)(2,1)S(1)} %get-tuple-element.38.refs_3_.refs_1_), channel_id=1, source_target_pairs={{0,16},{16,0},{1,17},{17,1},{2,18},{18,2},{3,19},{19,3},{4,20},{20... | collective-permute-start | bytes 786440 | tf_op jit(solution)/shard_map/ppermute | solution.py:297
  23.8 2.0 %collective-permute-start.9 = (bf16[256,512]{1,0:T(8,128)(2,1)S(1)}, bf16[256,512]{1,0:T(8,128)(2,1)S(1)}, u32[]{:S(2)}, u32[]{:S(2)}) collective-permute-start(bf16[256,512]{1,0:T(8,128)(2,1)S(1)} %get-tuple-element.39.refs_4_.refs_2_), channel_id=1, source_target_pairs={{0,16},{16,0},{1,17},{17,1},{2,18},{18,2},{3,19},{19,3},{4,20},{20... | collective-permute-start | bytes 786440 | tf_op jit(solution)/shard_map/ppermute | solution.py:297
  24.3 1.9 %collective-permute-start.12 = (bf16[256,512]{1,0:T(8,128)(2,1)S(1)}, bf16[256,512]{1,0:T(8,128)(2,1)S(1)}, u32[]{:S(2)}, u32[]{:S(2)}) collective-permute-start(bf16[256,512]{1,0:T(8,128)(2,1)S(1)} %collective-permute-done.4.refs_7_.refs_5_), channel_id=1, source_target_pairs={{0,16},{16,0},{1,17},{17,1},{2,18},{18,2},{3,19},{19,3},{4,20},{20... | collective-permute-start | bytes 786440 | tf_op jit(solution)/shard_map/ppermute | solution.py:297
  24.7 1.9 %collective-permute-start.13 = (bf16[256,512]{1,0:T(8,128)(2,1)S(1)}, bf16[256,512]{1,0:T(8,128)(2,1)S(1)}, u32[]{:S(2)}, u32[]{:S(2)}) collective-permute-start(bf16[256,512]{1,0:T(8,128)(2,1)S(1)} %collective-permute-done.5.refs_8_.refs_6_), channel_id=1, source_target_pairs={{0,16},{16,0},{1,17},{17,1},{2,18},{18,2},{3,19},{19,3},{4,20},{20... | collective-permute-start | bytes 786440 | tf_op jit(solution)/shard_map/ppermute | solution.py:297
  25.1 1.9 %collective-permute-start.14 = (bf16[256,512]{1,0:T(8,128)(2,1)S(1)}, bf16[256,512]{1,0:T(8,128)(2,1)S(1)}, u32[]{:S(2)}, u32[]{:S(2)}) collective-permute-start(bf16[256,512]{1,0:T(8,128)(2,1)S(1)} %collective-permute-done.6.refs_9_.refs_7_), channel_id=1, source_target_pairs={{0,16},{16,0},{1,17},{17,1},{2,18},{18,2},{3,19},{19,3},{4,20},{20... | collective-permute-start | bytes 786440 | tf_op jit(solution)/shard_map/ppermute | solution.py:297
  27.9 7.5 %collective-permute-start.15 = (f32[16,512]{1,0:T(8,128)S(1)}, f32[16,512]{1,0:T(8,128)S(1)}, u32[]{:S(2)}, u32[]{:S(2)}) collective-permute-start(f32[16,512]{1,0:T(8,128)S(1)} %get-tuple-element.49), channel_id=1, source_target_pairs={{0,1},{1,0},{2,3},{3,2},{4,5},{5,4},{6,7},{7,6},{8,9},{9,8},{10,11... | collective-permute-start | bytes 98312 | tf_op jit(solution)/shard_map/ppermute | solution.py:345
  29.7 5.7 %collective-permute-start.16 = (f32[16,512]{1,0:T(8,128)S(1)}, f32[16,512]{1,0:T(8,128)S(1)}, u32[]{:S(2)}, u32[]{:S(2)}) collective-permute-start(f32[16,512]{1,0:T(8,128)S(1)} %get-tuple-element.50), channel_id=1, source_target_pairs={{0,2},{1,3},{2,0},{3,1},{4,6},{5,7},{6,4},{7,5},{8,10},{9,11},{10,... | collective-permute-start | bytes 98312 | tf_op jit(solution)/shard_map/ppermute | solution.py:345
  29.8 6.3 %collective-permute-start.17 = (f32[16,512]{1,0:T(8,128)S(1)}, f32[16,512]{1,0:T(8,128)S(1)}, u32[]{:S(2)}, u32[]{:S(2)}) collective-permute-start(f32[16,512]{1,0:T(8,128)S(1)} %get-tuple-element.51), channel_id=1, source_target_pairs={{0,3},{1,2},{2,1},{3,0},{4,7},{5,6},{6,5},{7,4},{8,11},{9,10},{10,... | collective-permute-start | bytes 98312 | tf_op jit(solution)/shard_map/ppermute | solution.py:345
  33.0 11.9 %copy-start.1 = (f32[1,1024]{1,0:T(1,128)S(1)}, f32[1,1024]{1,0:T(1,128)}, u32[]{:S(2)}) copy-start(f32[1,1024]{1,0:T(1,128)} %scale_ref.1) | copy-start | bytes 12292
  36.2 11.3 %collective-permute-start.18 = (f32[16,512]{1,0:T(8,128)S(1)}, f32[16,512]{1,0:T(8,128)S(1)}, u32[]{:S(2)}, u32[]{:S(2)}) collective-permute-start(f32[16,512]{1,0:T(8,128)S(1)} %add_add_fusion.1), channel_id=1, source_target_pairs={{0,8},{1,9},{2,10},{3,11},{4,12},{5,13},{6,14},{7,15},{8,0},{9,1},... | collective-permute-start | bytes 98312 | tf_op jit(solution)/shard_map/ppermute | solution.py:345
  43.4 5.2 %collective-permute-start.19 = (f32[16,512]{1,0:T(8,128)S(1)}, f32[16,512]{1,0:T(8,128)S(1)}, u32[]{:S(2)}, u32[]{:S(2)}) collective-permute-start(f32[16,512]{1,0:T(8,128)S(1)} %add_add_fusion.1), channel_id=1, source_target_pairs={{0,4},{1,5},{2,6},{3,7},{4,0},{5,1},{6,2},{7,3},{8,12},{9,13},{10,... | collective-permute-start | bytes 98312 | tf_op jit(solution)/shard_map/ppermute | solution.py:345
  44.9 6.0 %collective-permute-start.20 = (f32[16,512]{1,0:T(8,128)S(1)}, f32[16,512]{1,0:T(8,128)S(1)}, u32[]{:S(2)}, u32[]{:S(2)}) collective-permute-start(f32[16,512]{1,0:T(8,128)S(1)} %add_add_fusion.1), channel_id=1, source_target_pairs={{0,12},{1,13},{2,14},{3,15},{4,8},{5,9},{6,10},{7,11},{8,4},{9,5},... | collective-permute-start | bytes 98312 | tf_op jit(solution)/shard_map/ppermute | solution.py:345
  62.3 2.7 %collective-permute-start.22 = (bf16[4,512,256]{2,1,0:T(8,128)(2,1)S(1)}, bf16[4,512,256]{2,1,0:T(8,128)(2,1)S(1)}, u32[]{:S(2)}, u32[]{:S(2)}) collective-permute-start(bf16[4,512,256]{2,1,0:T(8,128)(2,1)S(1)} %get-tuple-element.56), channel_id=1, source_target_pairs={{0,16},{16,0},{1,17},{17,1},{2,18},{18,2},{3,19},{19,3},{4,20},{20... | collective-permute-start | bytes 3145736 | tf_op jit(solution)/shard_map/ppermute | solution.py:297
  63.7 2.9 %collective-permute-start.21 = (bf16[4,512,256]{2,1,0:T(8,128)(2,1)S(1)}, bf16[4,512,256]{2,1,0:T(8,128)(2,1)S(1)}, u32[]{:S(2)}, u32[]{:S(2)}) collective-permute-start(bf16[4,512,256]{2,1,0:T(8,128)(2,1)S(1)} %back.1), channel_id=1, source_target_pairs={{0,16},{16,0},{1,17},{17,1},{2,18},{18,2},{3,19},{19,3},{4,20},{20... | collective-permute-start | bytes 3145736 | tf_op jit(solution)/shard_map/ppermute | solution.py:297

commit v2 on v1

--- a/solution.py
+++ b/solution.py
@@ -376,7 +376,7 @@
     mine = [*pin([here, beside, behind, ahead, across], left_1), *corners]
     theirs = [swap(block) for block in mine]
     keep, *others = project(own_fold, other_fold, mine, theirs)
-    received = trade(others, NEAR)
+    received = trade(others[::-1], NEAR[::-1])
     first, token_1 = load_first(own, mine)
     scaled, token_2 = load_second(other, theirs, first, interior_scale)
     keep = total(keep, received, token_1)

time: 134 us -> 134 us (level)
  no operation moved by 1% of the time
where the time goes in v2:
time: 134 us; the launch traced here: 133 us
  blocking collectives  74.1 us (55%)
  starting transfers between devices  28.3 us (21%)
  Pallas kernels  19.5 us (15%)
  waiting for transfers between devices  9.63 us (7%)
    all_to_all x4, blocking collectives, exchange(): return lax.all_to_all(value, axes, 0, 0, tiled=True)  74.1 us
    ppermute x7, starting transfers between devices, shift(): return lax.ppermute(value, ('x', 'yl', 'yh'), pairs)  13.3 us
    ppermute x6, starting transfers between devices, trade(): received.append(lax.ppermute(value, (*LAYERS, 'yh'), pairs))  12.9 us
    pallas_call x7, Pallas kernels, inside(): pl.pallas_call(kernel, out_shape=out_shape, in_specs=[INSIDE] * len(opera...  11.3 us
    pallas_call x2, Pallas kernels, mask(): pl.pallas_call(functools.partial(mask_kernel, tile=tile, last=last), out_...  8.1 us
    ppermute x6, waiting for transfers between devices, trade(): received.append(lax.ppermute(value, (*LAYERS, 'yh'), pairs))  4.63 us
    ppermute x10, waiting for transfers between devices, swap(): return lax.ppermute(value, 'c', [(0, 1), (1, 0)])  3.72 us
  transfers between devices with their start and end apart: 23, of which 14 were waited for; matrix products, arithmetic and copies ran while one was open for 0% of the time, Pallas kernels for 12%

profile of v2, /device:TPU:32, one launch (start us, length us, event | category | flops | bytes accessed | tf_op | source)
XLA Modules:
  0.0 133.3 jit_solution(16654896815918260082)
XLA Ops:
  0.0 0.0 copy-start
  0.0 3.0 %collective-permute-start = (bf16[256,512]{1,0:T(8,128)(2,1)}, bf16[256,512]{1,0:T(8,128)(2,1)S(1)}, u32[]{:S(2)}, u32[]{:S(2)}) collective-permute-start(bf16[256,512]{1,0:T(8,128)(2,1)} %param.8), channel_id=1, source_target_pairs={{0,128},{1,129},{32,160},{33,161},{64,192},{65,193},{96,224},{97,2... | collective-permute-start | bytes 786440 | tf_op jit(solution)/shard_map/ppermute | solution.py:328
  3.0 1.6 %collective-permute-start.1 = (bf16[256,512]{1,0:T(8,128)(2,1)}, bf16[256,512]{1,0:T(8,128)(2,1)S(1)}, u32[]{:S(2)}, u32[]{:S(2)}) collective-permute-start(bf16[256,512]{1,0:T(8,128)(2,1)} %param.8), channel_id=1, source_target_pairs={{0,32},{1,33},{32,0},{33,1},{64,96},{65,97},{96,64},{97,65},{128,1... | collective-permute-start | bytes 786440 | tf_op jit(solution)/shard_map/ppermute | solution.py:328
  4.6 0.6 collective-permute-start.2
  5.2 2.6 %collective-permute-start.3 = (bf16[256,512]{1,0:T(8,128)(2,1)}, bf16[256,512]{1,0:T(8,128)(2,1)S(1)}, u32[]{:S(2)}, u32[]{:S(2)}) collective-permute-start(bf16[256,512]{1,0:T(8,128)(2,1)} %param.8), channel_id=1, source_target_pairs={{0,192},{1,193},{32,224},{33,225},{64,0},{65,1},{96,32},{97,33},{1... | collective-permute-start | bytes 786440 | tf_op jit(solution)/shard_map/ppermute | solution.py:328
  7.8 4.0 %mask.2 = (bf16[512,2048]{1,0:T(8,128)(2,1)S(1)}, bf16[512,2048]{1,0:T(8,128)(2,1)S(1)}, bf16[192,512]{1,0:T(8,128)(2,1)S(1)}, f32[2,64,2048]{2,1,0:T(8,128)S(1)}) custom-call(s32[2,16]{1,0:T(2,128)} %bitcast.23, s32[2]{0:T(128)} %bitcast.25, bf16[1024,4096]{1,0:T(8,128)(2,1)} %bitcast.15, bf16[64,1024]{1,0:T(8,128)(2,1)} %bitcast.19, bf16[64,1024]{1,0:T(8,128)(2,1)} %bitcast.21), custom_call_target="tpu_custom_call" | custom-call | flops 268435456 | bytes 8388608 | tf_op jit(solution)/shard_map/mask/pallas_call | solution.py:192
  11.8 0.0 collective-permute-done.refs_0_
  11.9 0.0 collective-permute-done.1.refs_1_
  11.9 0.6 collective-permute-start.4
  12.5 2.7 %collective-permute-start.5 = (bf16[256,512]{1,0:T(8,128)(2,1)S(1)}, bf16[256,512]{1,0:T(8,128)(2,1)S(1)}, u32[]{:S(2)}, u32[]{:S(2)}) collective-permute-start(bf16[256,512]{1,0:T(8,128)(2,1)S(1)} %get-tuple-element.33.refs_1_), channel_id=1, source_target_pairs={{0,192},{1,193},{32,224},{33,225},{64,0},{65,1},{96,32},{97,33},{1... | collective-permute-start | bytes 786440 | tf_op jit(solution)/shard_map/ppermute | solution.py:328
  15.2 2.1 %collective-permute-start.6 = (bf16[256,512]{1,0:T(8,128)(2,1)S(1)}, bf16[256,512]{1,0:T(8,128)(2,1)S(1)}, u32[]{:S(2)}, u32[]{:S(2)}) collective-permute-start(bf16[256,512]{1,0:T(8,128)(2,1)S(1)} %get-tuple-element.35.refs_4_), channel_id=1, source_target_pairs={{0,33},{1,32},{32,1},{33,0},{64,97},{65,96},{96,65},{97,64},{128,1... | collective-permute-start | bytes 786440 | tf_op jit(solution)/shard_map/ppermute | solution.py:328
  17.3 0.0 copy-done.2
  17.4 4.1 %mask.3 = (bf16[512,2048]{1,0:T(8,128)(2,1)S(1)}, bf16[512,2048]{1,0:T(8,128)(2,1)S(1)}, bf16[192,512]{1,0:T(8,128)(2,1)S(1)}, bf16[192,2048]{1,0:T(8,128)(2,1)S(1)}, bf16[192,2048]{1,0:T(8,128)(2,1)S(1)}) custom-call(s32[2,16]{1,0:T(2,128)} %bitcast.24, s32[2]{0:T(128)} %bitcast.26, bf16[1024,4096]{1,0:T(8,128)(2,1)} %bitcast.16, ...), custom_call_target="tpu_custom_call" | custom-call | flops 268435456 | bytes 8388608 | tf_op jit(solution)/shard_map/mask/pallas_call | solution.py:192
  21.5 0.0 collective-permute-done.2.refs_2_
  21.5 0.0 collective-permute-done.3.refs_3_
  21.5 0.0 collective-permute-done.4.refs_7_.refs_5_
  21.5 0.0 collective-permute-done.5.refs_8_.refs_6_
  21.5 1.3 collective-permute-done.6.refs_9_.refs_7_
  22.8 0.0 collective-permute-start.10
  22.8 0.5 collective-permute-start.11
  23.3 0.0 collective-permute-start.7
  23.3 0.5 collective-permute-start.8
  23.8 0.0 collective-permute-start.9
  23.8 0.5 collective-permute-done.10.refs_5_.refs_11_
  24.3 0.1 collective-permute-start.12
  24.5 0.2 collective-permute-done.11.refs_6_.refs_12_
  24.7 0.1 collective-permute-start.13
  24.8 0.2 collective-permute-done.7.refs_2_.refs_8_
  25.1 0.1 collective-permute-start.14
  25.2 0.2 collective-permute-done.8.refs_3_.refs_9_
  25.4 0.4 collective-permute-done.9.refs_4_.refs_10_
  25.8 0.4 collective-permute-done.12.refs_7_.refs_13_
  26.2 0.4 collective-permute-done.13.refs_8_.refs_14_
  26.6 0.4 collective-permute-done.14.refs_9_.refs_15_
  26.9 1.0 project.1
  27.9 1.3 collective-permute-start.15
  29.3 1.9 %collective-permute-start.16 = (f32[16,512]{1,0:T(8,128)S(1)}, f32[16,512]{1,0:T(8,128)S(1)}, u32[]{:S(2)}, u32[]{:S(2)}) collective-permute-start(f32[16,512]{1,0:T(8,128)S(1)} %get-tuple-element.50), channel_id=1, source_target_pairs={{0,2},{1,3},{2,0},{3,1},{4,6},{5,7},{6,4},{7,5},{8,10},{9,11},{10,... | collective-permute-start | bytes 98312 | tf_op jit(solution)/shard_map/ppermute | solution.py:345
  31.2 1.8 %collective-permute-start.17 = (f32[16,512]{1,0:T(8,128)S(1)}, f32[16,512]{1,0:T(8,128)S(1)}, u32[]{:S(2)}, u32[]{:S(2)}) collective-permute-start(f32[16,512]{1,0:T(8,128)S(1)} %get-tuple-element.51), channel_id=1, source_target_pairs={{0,1},{1,0},{2,3},{3,2},{4,5},{5,4},{6,7},{7,6},{8,9},{9,8},{10,11... | collective-permute-start | bytes 98312 | tf_op jit(solution)/shard_map/ppermute | solution.py:345
  33.0 2.4 %load_first.1 = (f32[1024,512]{1,0:T(8,128)S(1)}, f32[16,512]{1,0:T(8,128)S(1)}) custom-call(bf16[512,2048]{1,0:T(8,128)(2,1)S(1)} %get-tuple-element.31.refs_0_, bf16[512,2048]{1,0:T(8,128)(2,1)S(1)} %get-tuple-element.34.refs_1_, bf16[256,512]{1,0:T(8,128)(2,1)S(1)} %get-tuple-element.37.refs_2_.refs_0_, ...), custom_call_target="tpu_custom_call" | custom-call | flops 2147483648 | bytes 1048576 | tf_op jit(solution)/shard_map/load_first/pallas_call | solution.py:217
  35.4 0.0 collective-permute-done.15
  35.4 0.0 collective-permute-done.16
  35.4 1.2 collective-permute-done.17
  36.6 6.4 %collective-permute-start.18 = (f32[16,512]{1,0:T(8,128)S(1)}, f32[16,512]{1,0:T(8,128)S(1)}, u32[]{:S(2)}, u32[]{:S(2)}) collective-permute-start(f32[16,512]{1,0:T(8,128)S(1)} %add_add_fusion.1), channel_id=1, source_target_pairs={{0,8},{1,9},{2,10},{3,11},{4,12},{5,13},{6,14},{7,15},{8,0},{9,1},... | collective-permute-start | bytes 98312 | tf_op jit(solution)/shard_map/ppermute | solution.py:345
  43.0 1.5 %collective-permute-start.19 = (f32[16,512]{1,0:T(8,128)S(1)}, f32[16,512]{1,0:T(8,128)S(1)}, u32[]{:S(2)}, u32[]{:S(2)}) collective-permute-start(f32[16,512]{1,0:T(8,128)S(1)} %add_add_fusion.1), channel_id=1, source_target_pairs={{0,4},{1,5},{2,6},{3,7},{4,0},{5,1},{6,2},{7,3},{8,12},{9,13},{10,... | collective-permute-start | bytes 98312 | tf_op jit(solution)/shard_map/ppermute | solution.py:345
  44.5 0.0 collective-permute-start.20
  44.5 2.6 %load_second.1 = (f32[512,1024]{1,0:T(8,128)S(1)}, f32[16,512]{1,0:T(8,128)S(1)}) custom-call(f32[1024,512]{1,0:T(8,128)S(1)} %get-tuple-element.42.first_ref, f32[1,1024]{1,0:T(1,128)S(1)} %copy-done.1, bf16[512,2048]{1,0:T(8,128)(2,1)S(1)} %get-tuple-element.43.refs_0_.refs_2_, bf16[512,2048]{1,0:T(8,128)(2,1)S(1)} %get-tuple-element.44.refs_1_.refs_3_, ...), custom_call_target="tpu_custom_call" | custom-call | flops 2147483648 | bytes 1048576 | tf_op jit(solution)/shard_map/load_second/pallas_call | solution.py:217
  47.0 0.0 collective-permute-done.18
  47.1 1.1 collective-permute-done.19
  48.2 2.3 %collective-permute-done.20 = f32[16,512]{1,0:T(8,128)S(1)} collective-permute-done((f32[16,512]{1,0:T(8,128)S(1)}, f32[16,512]{1,0:T(8,128)S(1)}, u32[]{:S(2)}, u32[]{:S(2)}) %collective-permute-start.20) | collective-permute-done | bytes 32800 | tf_op jit(solution)/shard_map/ppermute | solution.py:345
  50.5 9.8 %all_to_all.20 = f32[4,16,512]{2,1,0:T(8,128)S(1)} all-to-all(f32[4,16,512]{2,1,0:T(8,128)S(1)} %broadcast_in_dim.4), channel_id=1, replica_groups=mesh['x'=4,'yl'=2,'c'=2,'zh'=4,'zl'=2,'yh'=2] {'zl','yh'}, dimensions={0} | all-to-all | bytes 262144 | tf_op jit(solution)/shard_map/all_to_all | solution.py:293
  60.3 1.6 %solve_back.1 = (bf16[512,1024]{1,0:T(8,128)(2,1)S(1)}, bf16[4,512,256]{2,1,0:T(8,128)(2,1)S(1)}) custom-call(f32[512,1024]{1,0:T(8,128)S(1)} %get-tuple-element.45.scaled_ref, f32[64,512]{1,0:T(8,128)S(1)} %bitcast.14, bf16[192,512]{1,0:T(8,128)(2,1)S(1)} %get-tuple-element.54.refs_0_, bf16[192,512]{1,0:T(8,128)(2,1)S(1)} %get-tuple-element.36.refs_5_.refs_1_, ...), custom_call_target="tpu_custom_call" | custom-call | flops 1073741824 | bytes 1048576 | tf_op jit(solution)/shard_map/solve_back/pallas_call | solution.py:217
  61.9 0.1 collective-permute-start.22
  62.0 1.2 back.1
  63.3 0.6 collective-permute-start.21
  63.8 0.8 collective-permute-done.22.refs_2_
  64.6 1.3 back_add.2.refs_3_
  65.9 0.2 collective-permute-done.21.refs_2_
  66.1 1.3 back_add.3
  67.4 32.0 %all_to_all.21 = bf16[16,256,256]{2,1,0:T(8,128)(2,1)S(1)} all-to-all(bf16[16,256,256]{2,1,0:T(8,128)(2,1)S(1)} %bitcast.13), channel_id=1, replica_groups=mesh['x'=4,'yl'=2,'c'=2,'zh'=4,'zl'=2,'yh'=2] {'x','yl','yh'}, dimensions={0} | all-to-all | bytes 4194304 | tf_op jit(solution)/shard_map/all_to_all | solution.py:293
  99.4 0.3 convert_reduce_fusion
  99.7 13.7 %all_to_all.22 = f32[8,32,256]{2,1,0:T(8,128)S(1)} all-to-all(f32[8,32,256]{2,1,0:T(8,128)S(1)} %bitcast.18), channel_id=1, replica_groups=mesh['x'=4,'yl'=2,'c'=2,'zh'=4,'zl'=2,'yh'=2] {'zh','zl'}, dimensions={0} | all-to-all | bytes 524288 | tf_op jit(solution)/shard_map/all_to_all | solution.py:293
  113.5 18.6 %all_to_all.23 = f32[16,32,256]{2,1,0:T(8,128)S(1)} all-to-all(f32[16,32,256]{2,1,0:T(8,128)S(1)} %broadcast_in_dim.5), channel_id=1, replica_groups=mesh['x'=4,'yl'=2,'c'=2,'zh'=4,'zl'=2,'yh'=2] {'yh','zh','zl'}, dimensions={0} | all-to-all | bytes 1048576 | tf_op jit(solution)/shard_map/all_to_all | solution.py:293
  132.1 0.2 copy.18
  132.3 1.0 convolution_subtract_fusion
  (12 shorter events, 0.1 us)
Async XLA Ops:
  0.0 132.3 %copy-start = (bf16[256,256]{1,0:T(8,128)(2,1)S(1)}, bf16[256,256]{1,0:T(8,128)(2,1)}, u32[]{:S(2)}) copy-start(bf16[256,256]{1,0:T(8,128)(2,1)} %param.9) | copy-start | bytes 393220
  0.0 11.8 %collective-permute-start = (bf16[256,512]{1,0:T(8,128)(2,1)}, bf16[256,512]{1,0:T(8,128)(2,1)S(1)}, u32[]{:S(2)}, u32[]{:S(2)}) collective-permute-start(bf16[256,512]{1,0:T(8,128)(2,1)} %param.8), channel_id=1, source_target_pairs={{0,128},{1,129},{32,160},{33,161},{64,192},{65,193},{96,224},{97,2... | collective-permute-start | bytes 786440 | tf_op jit(solution)/shard_map/ppermute | solution.py:328
  3.0 8.8 %collective-permute-start.1 = (bf16[256,512]{1,0:T(8,128)(2,1)}, bf16[256,512]{1,0:T(8,128)(2,1)S(1)}, u32[]{:S(2)}, u32[]{:S(2)}) collective-permute-start(bf16[256,512]{1,0:T(8,128)(2,1)} %param.8), channel_id=1, source_target_pairs={{0,32},{1,33},{32,0},{33,1},{64,96},{65,97},{96,64},{97,65},{128,1... | collective-permute-start | bytes 786440 | tf_op jit(solution)/shard_map/ppermute | solution.py:328
  4.6 16.9 %collective-permute-start.2 = (bf16[256,512]{1,0:T(8,128)(2,1)}, bf16[256,512]{1,0:T(8,128)(2,1)S(1)}, u32[]{:S(2)}, u32[]{:S(2)}) collective-permute-start(bf16[256,512]{1,0:T(8,128)(2,1)} %param.8), channel_id=1, source_target_pairs={{0,64},{1,65},{32,96},{33,97},{64,128},{65,129},{96,160},{97,161},... | collective-permute-start | bytes 786440 | tf_op jit(solution)/shard_map/ppermute | solution.py:328
  5.2 16.3 %collective-permute-start.3 = (bf16[256,512]{1,0:T(8,128)(2,1)}, bf16[256,512]{1,0:T(8,128)(2,1)S(1)}, u32[]{:S(2)}, u32[]{:S(2)}) collective-permute-start(bf16[256,512]{1,0:T(8,128)(2,1)} %param.8), channel_id=1, source_target_pairs={{0,192},{1,193},{32,224},{33,225},{64,0},{65,1},{96,32},{97,33},{1... | collective-permute-start | bytes 786440 | tf_op jit(solution)/shard_map/ppermute | solution.py:328
  7.8 9.5 %copy-start.2 = (bf16[256,512]{1,0:T(8,128)(2,1)S(1)}, bf16[256,512]{1,0:T(8,128)(2,1)}, u32[]{:S(2)}) copy-start(bf16[256,512]{1,0:T(8,128)(2,1)} %param.8) | copy-start | bytes 786436
  11.9 9.6 %collective-permute-start.4 = (bf16[256,512]{1,0:T(8,128)(2,1)S(1)}, bf16[256,512]{1,0:T(8,128)(2,1)S(1)}, u32[]{:S(2)}, u32[]{:S(2)}) collective-permute-start(bf16[256,512]{1,0:T(8,128)(2,1)S(1)} %get-tuple-element.33.refs_1_), channel_id=1, source_target_pairs={{0,64},{1,65},{32,96},{33,97},{64,128},{65,129},{96,160},{97,161},... | collective-permute-start | bytes 786440 | tf_op jit(solution)/shard_map/ppermute | solution.py:328
  12.5 9.1 %collective-permute-start.5 = (bf16[256,512]{1,0:T(8,128)(2,1)S(1)}, bf16[256,512]{1,0:T(8,128)(2,1)S(1)}, u32[]{:S(2)}, u32[]{:S(2)}) collective-permute-start(bf16[256,512]{1,0:T(8,128)(2,1)S(1)} %get-tuple-element.33.refs_1_), channel_id=1, source_target_pairs={{0,192},{1,193},{32,224},{33,225},{64,0},{65,1},{96,32},{97,33},{1... | collective-permute-start | bytes 786440 | tf_op jit(solution)/shard_map/ppermute | solution.py:328
  15.2 7.6 %collective-permute-start.6 = (bf16[256,512]{1,0:T(8,128)(2,1)S(1)}, bf16[256,512]{1,0:T(8,128)(2,1)S(1)}, u32[]{:S(2)}, u32[]{:S(2)}) collective-permute-start(bf16[256,512]{1,0:T(8,128)(2,1)S(1)} %get-tuple-element.35.refs_4_), channel_id=1, source_target_pairs={{0,33},{1,32},{32,1},{33,0},{64,97},{65,96},{96,65},{97,64},{128,1... | collective-permute-start | bytes 786440 | tf_op jit(solution)/shard_map/ppermute | solution.py:328
  22.8 1.5 %collective-permute-start.10 = (bf16[256,512]{1,0:T(8,128)(2,1)S(1)}, bf16[256,512]{1,0:T(8,128)(2,1)S(1)}, u32[]{:S(2)}, u32[]{:S(2)}) collective-permute-start(bf16[256,512]{1,0:T(8,128)(2,1)S(1)} %get-tuple-element.40.refs_5_.refs_3_), channel_id=1, source_target_pairs={{0,16},{16,0},{1,17},{17,1},{2,18},{18,2},{3,19},{19,3},{4,20},{20... | collective-permute-start | bytes 786440 | tf_op jit(solution)/shard_map/ppermute | solution.py:297
  22.8 1.9 %collective-permute-start.11 = (bf16[256,512]{1,0:T(8,128)(2,1)S(1)}, bf16[256,512]{1,0:T(8,128)(2,1)S(1)}, u32[]{:S(2)}, u32[]{:S(2)}) collective-permute-start(bf16[256,512]{1,0:T(8,128)(2,1)S(1)} %get-tuple-element.41.refs_6_.refs_4_), channel_id=1, source_target_pairs={{0,16},{16,0},{1,17},{17,1},{2,18},{18,2},{3,19},{19,3},{4,20},{20... | collective-permute-start | bytes 786440 | tf_op jit(solution)/shard_map/ppermute | solution.py:297
  23.3 1.8 %collective-permute-start.7 = (bf16[256,512]{1,0:T(8,128)(2,1)S(1)}, bf16[256,512]{1,0:T(8,128)(2,1)S(1)}, u32[]{:S(2)}, u32[]{:S(2)}) collective-permute-start(bf16[256,512]{1,0:T(8,128)(2,1)S(1)} %get-tuple-element.37.refs_2_.refs_0_), channel_id=1, source_target_pairs={{0,16},{16,0},{1,17},{17,1},{2,18},{18,2},{3,19},{19,3},{4,20},{20... | collective-permute-start | bytes 786440 | tf_op jit(solution)/shard_map/ppermute | solution.py:297
  23.3 2.1 %collective-permute-start.8 = (bf16[256,512]{1,0:T(8,128)(2,1)S(1)}, bf16[256,512]{1,0:T(8,128)(2,1)S(1)}, u32[]{:S(2)}, u32[]{:S(2)}) collective-permute-start(bf16[256,512]{1,0:T(8,128)(2,1)S(1)} %get-tuple-element.38.refs_3_.refs_1_), channel_id=1, source_target_pairs={{0,16},{16,0},{1,17},{17,1},{2,18},{18,2},{3,19},{19,3},{4,20},{20... | collective-permute-start | bytes 786440 | tf_op jit(solution)/shard_map/ppermute | solution.py:297
  23.8 2.0 %collective-permute-start.9 = (bf16[256,512]{1,0:T(8,128)(2,1)S(1)}, bf16[256,512]{1,0:T(8,128)(2,1)S(1)}, u32[]{:S(2)}, u32[]{:S(2)}) collective-permute-start(bf16[256,512]{1,0:T(8,128)(2,1)S(1)} %get-tuple-element.39.refs_4_.refs_2_), channel_id=1, source_target_pairs={{0,16},{16,0},{1,17},{17,1},{2,18},{18,2},{3,19},{19,3},{4,20},{20... | collective-permute-start | bytes 786440 | tf_op jit(solution)/shard_map/ppermute | solution.py:297
  24.3 1.9 %collective-permute-start.12 = (bf16[256,512]{1,0:T(8,128)(2,1)S(1)}, bf16[256,512]{1,0:T(8,128)(2,1)S(1)}, u32[]{:S(2)}, u32[]{:S(2)}) collective-permute-start(bf16[256,512]{1,0:T(8,128)(2,1)S(1)} %collective-permute-done.4.refs_7_.refs_5_), channel_id=1, source_target_pairs={{0,16},{16,0},{1,17},{17,1},{2,18},{18,2},{3,19},{19,3},{4,20},{20... | collective-permute-start | bytes 786440 | tf_op jit(solution)/shard_map/ppermute | solution.py:297
  24.7 1.9 %collective-permute-start.13 = (bf16[256,512]{1,0:T(8,128)(2,1)S(1)}, bf16[256,512]{1,0:T(8,128)(2,1)S(1)}, u32[]{:S(2)}, u32[]{:S(2)}) collective-permute-start(bf16[256,512]{1,0:T(8,128)(2,1)S(1)} %collective-permute-done.5.refs_8_.refs_6_), channel_id=1, source_target_pairs={{0,16},{16,0},{1,17},{17,1},{2,18},{18,2},{3,19},{19,3},{4,20},{20... | collective-permute-start | bytes 786440 | tf_op jit(solution)/shard_map/ppermute | solution.py:297
  25.1 1.9 %collective-permute-start.14 = (bf16[256,512]{1,0:T(8,128)(2,1)S(1)}, bf16[256,512]{1,0:T(8,128)(2,1)S(1)}, u32[]{:S(2)}, u32[]{:S(2)}) collective-permute-start(bf16[256,512]{1,0:T(8,128)(2,1)S(1)} %collective-permute-done.6.refs_9_.refs_7_), channel_id=1, source_target_pairs={{0,16},{16,0},{1,17},{17,1},{2,18},{18,2},{3,19},{19,3},{4,20},{20... | collective-permute-start | bytes 786440 | tf_op jit(solution)/shard_map/ppermute | solution.py:297
  27.9 7.5 %collective-permute-start.15 = (f32[16,512]{1,0:T(8,128)S(1)}, f32[16,512]{1,0:T(8,128)S(1)}, u32[]{:S(2)}, u32[]{:S(2)}) collective-permute-start(f32[16,512]{1,0:T(8,128)S(1)} %get-tuple-element.49), channel_id=1, source_target_pairs={{0,3},{1,2},{2,1},{3,0},{4,7},{5,6},{6,5},{7,4},{8,11},{9,10},{10,... | collective-permute-start | bytes 98312 | tf_op jit(solution)/shard_map/ppermute | solution.py:345
  29.3 6.1 %collective-permute-start.16 = (f32[16,512]{1,0:T(8,128)S(1)}, f32[16,512]{1,0:T(8,128)S(1)}, u32[]{:S(2)}, u32[]{:S(2)}) collective-permute-start(f32[16,512]{1,0:T(8,128)S(1)} %get-tuple-element.50), channel_id=1, source_target_pairs={{0,2},{1,3},{2,0},{3,1},{4,6},{5,7},{6,4},{7,5},{8,10},{9,11},{10,... | collective-permute-start | bytes 98312 | tf_op jit(solution)/shard_map/ppermute | solution.py:345
  31.2 5.4 %collective-permute-start.17 = (f32[16,512]{1,0:T(8,128)S(1)}, f32[16,512]{1,0:T(8,128)S(1)}, u32[]{:S(2)}, u32[]{:S(2)}) collective-permute-start(f32[16,512]{1,0:T(8,128)S(1)} %get-tuple-element.51), channel_id=1, source_target_pairs={{0,1},{1,0},{2,3},{3,2},{4,5},{5,4},{6,7},{7,6},{8,9},{9,8},{10,11... | collective-permute-start | bytes 98312 | tf_op jit(solution)/shard_map/ppermute | solution.py:345
  33.0 11.4 %copy-start.1 = (f32[1,1024]{1,0:T(1,128)S(1)}, f32[1,1024]{1,0:T(1,128)}, u32[]{:S(2)}) copy-start(f32[1,1024]{1,0:T(1,128)} %scale_ref.1) | copy-start | bytes 12292
  36.6 10.4 %collective-permute-start.18 = (f32[16,512]{1,0:T(8,128)S(1)}, f32[16,512]{1,0:T(8,128)S(1)}, u32[]{:S(2)}, u32[]{:S(2)}) collective-permute-start(f32[16,512]{1,0:T(8,128)S(1)} %add_add_fusion.1), channel_id=1, source_target_pairs={{0,8},{1,9},{2,10},{3,11},{4,12},{5,13},{6,14},{7,15},{8,0},{9,1},... | collective-permute-start | bytes 98312 | tf_op jit(solution)/shard_map/ppermute | solution.py:345
  43.0 5.2 %collective-permute-start.19 = (f32[16,512]{1,0:T(8,128)S(1)}, f32[16,512]{1,0:T(8,128)S(1)}, u32[]{:S(2)}, u32[]{:S(2)}) collective-permute-start(f32[16,512]{1,0:T(8,128)S(1)} %add_add_fusion.1), channel_id=1, source_target_pairs={{0,4},{1,5},{2,6},{3,7},{4,0},{5,1},{6,2},{7,3},{8,12},{9,13},{10,... | collective-permute-start | bytes 98312 | tf_op jit(solution)/shard_map/ppermute | solution.py:345
  44.5 6.0 %collective-permute-start.20 = (f32[16,512]{1,0:T(8,128)S(1)}, f32[16,512]{1,0:T(8,128)S(1)}, u32[]{:S(2)}, u32[]{:S(2)}) collective-permute-start(f32[16,512]{1,0:T(8,128)S(1)} %add_add_fusion.1), channel_id=1, source_target_pairs={{0,12},{1,13},{2,14},{3,15},{4,8},{5,9},{6,10},{7,11},{8,4},{9,5},... | collective-permute-start | bytes 98312 | tf_op jit(solution)/shard_map/ppermute | solution.py:345
  61.9 2.7 %collective-permute-start.22 = (bf16[4,512,256]{2,1,0:T(8,128)(2,1)S(1)}, bf16[4,512,256]{2,1,0:T(8,128)(2,1)S(1)}, u32[]{:S(2)}, u32[]{:S(2)}) collective-permute-start(bf16[4,512,256]{2,1,0:T(8,128)(2,1)S(1)} %get-tuple-element.56), channel_id=1, source_target_pairs={{0,16},{16,0},{1,17},{17,1},{2,18},{18,2},{3,19},{19,3},{4,20},{20... | collective-permute-start | bytes 3145736 | tf_op jit(solution)/shard_map/ppermute | solution.py:297
  63.3 2.9 %collective-permute-start.21 = (bf16[4,512,256]{2,1,0:T(8,128)(2,1)S(1)}, bf16[4,512,256]{2,1,0:T(8,128)(2,1)S(1)}, u32[]{:S(2)}, u32[]{:S(2)}) collective-permute-start(bf16[4,512,256]{2,1,0:T(8,128)(2,1)S(1)} %back.1), channel_id=1, source_target_pairs={{0,16},{16,0},{1,17},{17,1},{2,18},{18,2},{3,19},{19,3},{4,20},{20... | collective-permute-start | bytes 3145736 | tf_op jit(solution)/shard_map/ppermute | solution.py:297
